TPU v7x, 256 devices: a whole 4x4x8 slice. The times are simulated.
256 devices in a mesh: branch: 32 (over z, x), head: 8 (over y, core).
Axes of the slice: x: 4, y: 4, z: 8, core: 2. Of those that a mesh axis runs over, the one named last changes fastest.
Arguments:
- query_nope: bfloat16 [3072, 16384], P('branch', 'head'), may hold values from -6 to 6
- query_rope: bfloat16 [3072, 8192], P('branch', 'head'), may hold values from -448 to 448
- key_up: bfloat16 [128, 128, 512], P('head'), may hold values from -0.5 to 0.5
- value_up: bfloat16 [128, 512, 128], P('head'), may hold values from -1.5 to 1.5
- out_weight: bfloat16 [16384, 7168], P('head', 'branch'), may hold values from -0.046875 to 0.046875
- block_pool: bfloat16 [768, 128, 576], P('branch'), may hold values from -6 to 6
- recent_blocks: bfloat16 [768, 128, 576], P('branch'), may hold values from -6 to 6
- new_latent: bfloat16 [3072, 576], P('branch'), may hold values from -6 to 6
- parent: int32 [768], P('branch'), may hold values from 0 to 767, as said below
- lengths: int32 [768], P('branch'), may hold values from 1 to 128
- block_table: int32 [768, 1], P('branch'), may hold values from 0 to 23, as said below
Outputs:
- mixed: bfloat16 [3072, 7168], P('head', 'branch')
Inputs may be any that keep to these rules, and one draw needn't show every extreme that they name: Children 2i and 2i+1 share one parent; of the 12 sibling pairs of one device at most 1 have parents on one device, and on every device some source device holds exactly 1 of its pairs' parents. Entries name pool blocks of the child's own device: block j of child b is block_pool row 24 * (b // 24) + block_table[b, j].
All inputs are finite; a program needn't handle non-finite values.
Results may differ from a plain program's by a relative error of at most 0.014.
Values may be sent and summed in bfloat16 or wider, within the bound.
A program may use at most 128 MiB of HBM per device.

v0:
```python
import jax
import jax.numpy as jnp
from jax import lax
from jax.sharding import PartitionSpec as P

NOPE = 128
ROPE = 64
LAT = 512
VDIM = 128
BLOCK = 128
STEPS = 4
B_DEV = 24
LOC = 1


def rank_among(sources):
    count = sources.shape[-1]
    earlier = jnp.arange(count)[:, None] < jnp.arange(count)[None, :]
    same_source = sources[..., :, None] == sources[..., None, :]
    return jnp.sum(same_source & earlier, axis=-2)


def local(
    query_nope,
    query_rope,
    key_up,
    value_up,
    out_weight,
    block_pool,
    recent_blocks,
    new_latent,
    parent,
    lengths,
    block_table,
):
    heads_here = key_up.shape[0]
    rows_here = query_nope.shape[0]
    width = LAT + ROPE
    groups = lax.axis_size("branch")
    slot_count = (B_DEV // 2 + groups - 1) // groups
    branch_index = lax.axis_index("branch")
    every_parent = lax.all_gather(parent, "branch", axis=0, tiled=True)
    child_parent = every_parent.reshape(groups, B_DEV)
    child_source = child_parent // B_DEV
    rank_within = rank_among(child_source)
    owned_here = child_source == branch_index
    slot_rows = []
    for slot_number in range(2 * slot_count):
        picked = owned_here & (rank_within == slot_number)
        slot_rows.append(jnp.sum(jnp.where(picked, child_parent % B_DEV, 0), axis=1))
    local_index = jnp.stack(slot_rows, axis=1)
    outgoing = recent_blocks[local_index]
    incoming = lax.all_to_all(outgoing, "branch", split_axis=0, concat_axis=0, tiled=True)
    source = parent // B_DEV
    own_rank = rank_among(source)
    forked_rows = incoming[source, own_rank]
    q_heads = query_nope.reshape(rows_here, heads_here, NOPE)
    q_latent = jnp.einsum(
        "rhn,hnl->rhl", q_heads, key_up, preferred_element_type=jnp.float32
    ).astype(jnp.bfloat16)
    query_vectors = jnp.concatenate(
        [q_latent, query_rope.reshape(rows_here, heads_here, ROPE)], axis=2
    )
    query_vectors = query_vectors.reshape(B_DEV, STEPS * heads_here, width)
    prefix_latent = block_pool[block_table].reshape(B_DEV, LOC * BLOCK, width)
    newly_drafted_keys = new_latent.reshape(B_DEV, STEPS, width)
    score_scale = (NOPE + ROPE) ** (-0.5)
    score_prefix = (
        jnp.einsum("dpy,diy->dpi", query_vectors, prefix_latent, preferred_element_type=jnp.float32)
        * score_scale
    )
    score_fork = (
        jnp.einsum("dpy,diy->dpi", query_vectors, forked_rows, preferred_element_type=jnp.float32)
        * score_scale
    )
    score_fresh = (
        jnp.einsum(
            "dpy,diy->dpi", query_vectors, newly_drafted_keys, preferred_element_type=jnp.float32
        )
        * score_scale
    )
    row_of = jnp.arange(LOC * BLOCK)
    allow_prefix = row_of[None, None, :] < lengths[:, None, None]
    query_step = jnp.arange(STEPS * heads_here) // heads_here
    allow_fresh = jnp.arange(STEPS)[None, None, :] <= query_step[None, :, None]
    score_prefix = jnp.where(allow_prefix, score_prefix, -jnp.inf)
    score_fresh = jnp.where(allow_fresh, score_fresh, -jnp.inf)
    row_peak = jnp.maximum(
        jnp.maximum(jnp.max(score_prefix, axis=2), jnp.max(score_fork, axis=2)),
        jnp.max(score_fresh, axis=2),
    )
    prefix_weight = jnp.exp(score_prefix - row_peak[:, :, None]).astype(jnp.bfloat16)
    branch_weight = jnp.exp(score_fork - row_peak[:, :, None]).astype(jnp.bfloat16)
    newest_weight = jnp.exp(score_fresh - row_peak[:, :, None]).astype(jnp.bfloat16)
    weight_sum = jnp.sum(prefix_weight.astype(jnp.float32), axis=2) + jnp.sum(
        branch_weight.astype(jnp.float32), axis=2
    )
    weight_sum = weight_sum + jnp.sum(newest_weight.astype(jnp.float32), axis=2)
    context_vectors = jnp.einsum(
        "stf,sfr->str", prefix_weight, prefix_latent, preferred_element_type=jnp.float32
    )
    context_vectors = context_vectors + jnp.einsum(
        "stf,sfr->str", branch_weight, forked_rows, preferred_element_type=jnp.float32
    )
    context_vectors = context_vectors + jnp.einsum(
        "stf,sfr->str", newest_weight, newly_drafted_keys, preferred_element_type=jnp.float32
    )
    context_vectors = (context_vectors[:, :, :LAT] / weight_sum[:, :, None]).astype(jnp.bfloat16)
    context_vectors = context_vectors.reshape(rows_here, heads_here, LAT)
    attended = jnp.einsum(
        "rhl,hlv->rhv", context_vectors, value_up, preferred_element_type=jnp.float32
    )
    attended = attended.astype(jnp.bfloat16).reshape(rows_here, heads_here * VDIM)
    partial_rows = jnp.dot(
        lax.all_gather(attended, "branch", axis=0, tiled=True),
        out_weight,
        preferred_element_type=jnp.float32,
    )
    mixed = lax.psum_scatter(partial_rows, "head", scatter_dimension=0, tiled=True)
    return mixed.astype(jnp.bfloat16)


def solution(mesh):
    return jax.shard_map(
        local,
        mesh=mesh,
        in_specs=(
            P("branch", "head"),
            P("branch", "head"),
            P("head", None, None),
            P("head", None, None),
            P("head", "branch"),
            P("branch", None, None),
            P("branch", None, None),
            P("branch", None),
            P("branch"),
            P("branch"),
            P("branch", None),
        ),
        out_specs=P("head", "branch"),
        check_vma=False,
    )
```

profile of v0, /device:TPU:18, one launch (start us, length us, event | category | flops | bytes accessed | tf_op | source)
XLA Modules:
  0.0 443.6 jit_solution(13609251150430091304)
XLA Ops:
  6.5 1.4 dynamic-slice
  8.6 0.9 dynamic-update-slice
  9.5 22.5 %all-reduce = s32[768]{0:T(1024)S(1)} all-reduce(s32[768]{0:T(1024)S(1)} %dynamic-update-slice), channel_id=1, replica_groups=mesh['branch'=32,'head'=8] {'branch'}, use_global_device_ids=true, to_apply=%add | all-reduce | flops 768 | bytes 6144
  35.3 1.4 copy.24
  42.3 6.0 %gather_fusion.1 = bf16[64,128,576]{1,2,0:T(8,128)(2,1)} fusion(bf16[24,128,576]{1,2,0:T(8,128)(2,1)S(1)} %copy-done, s32[1024]{0:T(1024)S(1)} %pad_clamp_fusion), kind=kCustom, calls=%fused_computation.1 | custom fusion | bytes 18874624 | tf_op jit(solution)/shard_map/gather | solution.py:52
  48.2 6.0 %all-to-all-start = ((bf16[32,2,128,576]{2,3,1,0:T(8,128)(2,1)}), bf16[32,2,128,576]{2,3,1,0:T(8,128)(2,1)}, u32[]{:S(2)}, u32[]{:S(2)}) async-start(bf16[32,2,128,576]{2,3,1,0:T(8,128)(2,1)} %bitcast.47), calls=%async_computation | async-start | bytes 18874368 | tf_op jit(solution)/shard_map/all_to_all | solution.py:53
  54.5 2.2 fusion.4
  56.7 2.0 copy.21
  58.7 1.0 concatenate.31
  60.5 3.2 gather_fusion
  64.0 3.0 fusion.29
  67.0 2.3 fusion.30
  69.3 185.3 %all-to-all-done = bf16[32,2,128,576]{2,3,1,0:T(8,128)(2,1)} async-done(((bf16[32,2,128,576]{2,3,1,0:T(8,128)(2,1)}), bf16[32,2,128,576]{2,3,1,0:T(8,128)(2,1)}, u32[]{:S(2)}, u32[]{:S(2)}) %all-to-all-start) | async-done | bytes 9437216 | tf_op jit(solution)/shard_map/all_to_all | solution.py:53
  254.6 6.6 %gather_fusion.2 = bf16[24,128,576]{1,2,0:T(8,128)(2,1)} fusion(bf16[32,2,128,576]{2,3,1,0:T(8,128)(2,1)} %all-to-all-done, s32[24]{0:T(128)S(1)} %fusion.24), kind=kCustom, calls=%fused_computation.2 | custom fusion | bytes 7078080 | tf_op jit(solution)/shard_map/gather | solution.py:56
  261.2 3.6 fusion.31
  264.9 1.4 fusion.16
  267.1 1.4 fusion.15
  270.0 1.0 copy-done.13
  271.0 2.0 fusion.9
  273.0 0.9 copy.45
  274.1 119.5 %all-gather.2.cloned.1.call-done = bf16[3072,2048]{1,0:T(8,128)(2,1)} async-done(((bf16[96,2048]{1,0:T(8,128)(2,1)}), bf16[3072,2048]{1,0:T(8,128)(2,1)}) %all-gather.2.cloned.1.call-update) | async-done | bytes 12582928 | tf_op jit(solution)/shard_map/all_gather | solution.py:115
  393.7 10.4 %fusion.32 = f32[3072,224]{0,1:T(8,128)} fusion(bf16[3072,2048]{1,0:T(8,128)(2,1)} %all-gather.2.cloned.1.call-done, bf16[2048,224]{0,1:T(8,128)(2,1)} %param.15), kind=kOutput, calls=%fused_computation.71 | convolution fusion | flops 2818572288 | bytes 16252928 | tf_op jit(solution)/shard_map/dot_general | solution.py:114
  404.0 31.1 %reduce-scatter.2.cloned.1.call-done = f32[384,224]{0,1:T(8,128)} async-done(((f32[3072,224]{0,1:T(8,128)}), f32[384,224]{0,1:T(8,128)}) %reduce-scatter.2.cloned.1.call-update) | async-done | bytes 344080 | tf_op jit(solution)/shard_map/reduce_scatter | solution.py:119
  435.1 1.7 convert_element_type.55
  (66 shorter events, 12.6 us)
Async XLA Ops:
  6.5 35.7 %copy-start = (bf16[24,128,576]{1,2,0:T(8,128)(2,1)S(1)}, bf16[24,128,576]{1,2,0:T(8,128)(2,1)}, u32[]{:S(2)}) copy-start(bf16[24,128,576]{1,2,0:T(8,128)(2,1)} %param.17) | copy-start | bytes 10616836
  48.2 6.3 %copy-start.7 = (bf16[96,2048]{1,0:T(8,128)(2,1)S(1)}, bf16[96,2048]{1,0:T(8,128)(2,1)}, u32[]{:S(2)}) copy-start(bf16[96,2048]{1,0:T(8,128)(2,1)} %param.11) | copy-start | bytes 1179652
  48.2 206.4 %all-to-all-start = ((bf16[32,2,128,576]{2,3,1,0:T(8,128)(2,1)}), bf16[32,2,128,576]{2,3,1,0:T(8,128)(2,1)}, u32[]{:S(2)}, u32[]{:S(2)}) async-start(bf16[32,2,128,576]{2,3,1,0:T(8,128)(2,1)} %bitcast.47), calls=%async_computation | async-start | bytes 18874368 | tf_op jit(solution)/shard_map/all_to_all | solution.py:53
  54.3 4.5 %copy-start.9 = (bf16[96,1024]{1,0:T(8,128)(2,1)S(1)}, bf16[96,1024]{1,0:T(8,128)(2,1)}, u32[]{:S(2)}) copy-start(bf16[96,1024]{1,0:T(8,128)(2,1)} %param.12) | copy-start | bytes 589828
  54.3 5.5 %copy-start.10 = (bf16[96,576]{1,0:T(8,128)(2,1)S(1)}, bf16[96,576]{1,0:T(8,128)(2,1)}, u32[]{:S(2)}) copy-start(bf16[96,576]{1,0:T(8,128)(2,1)} %param.18) | copy-start | bytes 331780
  54.3 6.2 %copy-start.14 = (s32[24,1]{0,1:T(1,128)S(1)}, s32[24,1]{0,1:T(1,128)}, u32[]{:S(2)}) copy-start(s32[24,1]{0,1:T(1,128)} %param.21) | copy-start | bytes 292
  54.3 339.4 %all-gather.2.cloned.1.call-start = ((), (), s32[]{:S(2)}) async-start(), calls=%async_computation.2 | async-start | bytes 12976128 | tf_op jit(solution)/shard_map/all_gather | solution.py:115
  60.5 3.3 copy-start.15
  60.5 3.4 copy-start.12
  63.8 3.2 copy-start.4
  63.8 3.2 copy-start.6
  261.2 3.7 copy-start.11
  261.2 3.7 copy-start.2
  264.9 1.4 copy-start.3
  267.1 1.4 copy-start.8
  267.1 1.5 copy-start.5
  269.4 1.6 copy-start.13
  273.9 161.3 %reduce-scatter.2.cloned.1.call-start = ((), (), s32[]{:S(2)}) async-start(), calls=%async_computation.3 | async-start | bytes 3096576 | tf_op jit(solution)/shard_map/reduce_scatter | solution.py:119
  393.7 43.1 %copy-start.1 = (bf16[24,128,576]{1,2,0:T(8,128)(2,1)S(1)}, bf16[24,128,576]{1,2,0:T(8,128)(2,1)}, u32[]{:S(2)}) copy-start(bf16[24,128,576]{1,2,0:T(8,128)(2,1)} %param.17) | copy-start | bytes 10616836
Sparse Core Ops, SparseCore 0:
  274.0 119.6 all-gather.1
  404.2 30.9 reduce-scatter.1
where the time goes:
time: 449 us; the launch traced here: 444 us
  waiting for transfers between devices  336 us (75%)
  local copies, waits for them, and re-layouts  30.1 us (7%)
  matrix products  27 us (6%)
  blocking collectives  22.5 us (5%)
  between operations  14.3 us (3%)
  other arithmetic  7.27 us (2%)
  starting transfers between devices  6.53 us (1%)
    all_to_all x1, waiting for transfers between devices, local(): lax.all_to_all(outgoing, 'branch', split_axis=0, concat_axis=0, tiled=True)  185 us
    all_gather x1, waiting for transfers between devices, local(): lax.all_gather(attended, 'branch', axis=0, tiled=True)  120 us
    reduce_scatter x1, waiting for transfers between devices, local(): lax.psum_scatter(partial_rows, 'head', scatter_dimension=0, tiled=True)  31.1 us
    unnamed x1, blocking collectives  22.5 us
    dot_general x1, matrix products, local(): jnp.dot(lax.all_gather(attended, 'branch', axis=0, tiled=True), out_weigh...  10.4 us
  transfers between devices with their start and end apart: 3, of which 3 were waited for; matrix products, arithmetic and copies ran while one was open for 3% of the time, Pallas kernels for 0%

commit v1 on v0

v1 whole, which is shorter than its diff:
```python
import functools

import jax
import jax.numpy as jnp
from jax import lax
from jax.experimental import pallas as pl
from jax.experimental.pallas import tpu as pltpu
from jax.sharding import PartitionSpec as P

NOPE = 128
ROPE = 64
LAT = 512
VDIM = 128
BLOCK = 128
STEPS = 4
B_DEV = 24
PAIRS = B_DEV // 2
WIDTH = LAT + ROPE
HEADS = 16
ROWS = B_DEV * STEPS
HALF = ROWS // 2
QROWS = ROWS * HEADS
COLS = 224
NZ, NX, NY = 8, 4, 4
GROUPS = NZ * NX
PART = 80
LANES = LAT // 128
SCALE = (NOPE + ROPE) ** -0.5
BF = jnp.bfloat16
F32 = jnp.float32
MESH = pl.DeviceIdType.MESH
NT = (((1,), (1,)), ((), ()))


def dot(a, b):
    return jnp.dot(a, b, preferred_element_type=F32)


def dot_nt(a, b):
    return lax.dot_general(a, b, NT, preferred_element_type=F32)


def remote(src, dst, send, recv, **where):
    return pltpu.make_async_remote_copy(
        src_ref=src, dst_ref=dst, send_sem=send, recv_sem=recv,
        device_id=where, device_id_type=MESH,
    )


def attend_kernel(
    par, lens, table,
    qn_hbm, qr_hbm, ku_hbm, vu_hbm, pool_hbm, recent_hbm, nl_hbm,
    att,
    qn, qr, ku, vu, pool, nl, nlt,
    qs, ctx, peak, total,
    mine, packed, slots, my_par, all_par, pick_v, pick_s, parts, fork,
    load_sem, pick_sem, par_send, par_recv, out_send, out_recv, ring_send, ring_recv, core_send, core_recv,
):
    me = lax.axis_index("branch")
    head = lax.axis_index("head")
    y, core = head // 2, lax.rem(head, 2)
    up, down = lax.rem(y + 1, NY), lax.rem(y + 3, NY)
    far = lax.rem(y + 2, NY)
    row0 = pl.multiple_of(y * 144 + core * 64, 16)

    loads = [
        pltpu.make_async_copy(recent_hbm.at[:, pl.ds(row0, PART), :], mine, load_sem.at[0]),
        pltpu.make_async_copy(ku_hbm, ku, load_sem.at[1]),
        pltpu.make_async_copy(qn_hbm, qn, load_sem.at[2]),
        pltpu.make_async_copy(pool_hbm, pool, load_sem.at[3]),
        pltpu.make_async_copy(qr_hbm, qr, load_sem.at[4]),
        pltpu.make_async_copy(nl_hbm, nl, load_sem.at[5]),
        pltpu.make_async_copy(vu_hbm, vu, load_sem.at[6]),
    ]
    for load in loads:
        load.start()

    barrier = pltpu.get_barrier_semaphore()

    def greet(i, _):
        pl.semaphore_signal(barrier, inc=1, device_id={"branch": lax.rem(me + i, GROUPS)}, device_id_type=MESH)
        return 0

    lax.fori_loop(1, GROUPS, greet, 0)
    for other in (up * 2 + core, down * 2 + core, y * 2 + 1 - core):
        pl.semaphore_signal(barrier, inc=1, device_id={"head": other}, device_id_type=MESH)

    lane = lax.broadcasted_iota(jnp.int32, (1, 128), 1)
    row = jnp.zeros((1, 128), jnp.int32) - 1
    for b in range(0, B_DEV, 2):
        row = jnp.where(lane == b, par[b], row)
    my_par[...] = row
    all_par[me] = row
    pl.semaphore_wait(barrier, GROUPS - 1 + 3)

    def par_copy(i):
        d = lax.rem(me + i, GROUPS)
        return remote(my_par, all_par.at[me], par_send.at[i], par_recv.at[me], branch=d)

    def start_par(i, _):
        par_copy(i).start()
        return 0

    lax.fori_loop(1, GROUPS, start_par, 0)

    loads[1].wait()
    loads[2].wait()
    for h in range(HEADS):
        q = dot(qn[:, h * NOPE:(h + 1) * NOPE], ku[h])
        q = q.astype(BF).astype(F32)
        for j in range(LANES):
            qs[j, pl.ds(h, ROWS, stride=HEADS), :] = q[:, j * 128:(j + 1) * 128]

    def wait_par(i, _):
        src = lax.rem(me + i, GROUPS)
        remote(my_par, all_par.at[src], par_send.at[i], par_recv.at[src], branch=src).wait()
        return 0

    lax.fori_loop(1, GROUPS, wait_par, 0)
    local = all_par[...] - me * B_DEV
    hit = (local >= 0) & (local < B_DEV)
    pick_v[...] = jnp.broadcast_to(
        jnp.sum(jnp.where(hit, local, 0), axis=2, keepdims=True), (GROUPS, 1, 128)
    )
    pick = pltpu.make_async_copy(pick_v, pick_s, pick_sem)
    pick.start()
    loads[0].wait()
    pick.wait()

    def send_block(i, _):
        d = lax.rem(me + i, GROUPS)
        packed[d] = mine[pick_s[d, 0, 0]]
        remote(packed.at[d], slots.at[me], out_send.at[d], out_recv.at[me], branch=d).start()
        return 0

    lax.fori_loop(1, GROUPS, send_block, 0)
    slots[me] = mine[pick_s[me, 0, 0]]

    loads[3].wait()
    loads[4].wait()
    loads[5].wait()
    nlt[...] = jnp.zeros_like(nlt)
    nlt[:, :ROWS] = nl[...].astype(F32).T.astype(BF)

    key = lax.broadcasted_iota(jnp.int32, (STEPS * HEADS, 256), 1)
    step = lax.broadcasted_iota(jnp.int32, (STEPS * HEADS, 256), 0) // HEADS

    def query(rows):
        return jnp.concatenate([qs[j, rows, :] for j in range(LANES)], axis=1).astype(BF)

    def prefix(b, _):
        rows = pl.ds(pl.multiple_of(b * 64, 64), 64)
        keys = jnp.concatenate([pool[table[b]], nlt[...]], axis=1)
        s = dot(query(rows), keys[:LAT]) + dot(qr[rows, :], keys[LAT:])
        fresh = key - BLOCK - b * STEPS
        allowed = (key < lens[b]) | ((fresh >= 0) & (fresh <= step))
        s = jnp.where(allowed, s * SCALE, -jnp.inf)
        m = jnp.max(s, axis=1, keepdims=True)
        w = jnp.exp(s - m).astype(BF)
        total[rows, :] = jnp.broadcast_to(jnp.sum(w.astype(F32), axis=1, keepdims=True), (64, 128))
        peak[rows, :] = jnp.broadcast_to(m, (64, 128))
        c = dot_nt(w, keys[:LAT])
        for j in range(LANES):
            ctx[j, rows, :] = c[:, j * 128:(j + 1) * 128]
        return 0

    lax.fori_loop(0, B_DEV // 2, prefix, 0)

    def wait_block(i, _):
        src = lax.rem(me + i, GROUPS)
        remote(packed.at[src], slots.at[src], out_send.at[src], out_recv.at[src], branch=src).wait()
        return 0

    lax.fori_loop(1, GROUPS, wait_block, 0)
    for p in range(PAIRS):
        parts[head, p] = slots[par[2 * p] // B_DEV]

    def piece(h, half):
        at = parts.at[h]
        return at if half is None else at.at[pl.ds(half * (PAIRS // 2), PAIRS // 2)]

    def ring(n, h, half, to):
        return remote(piece(h, half), piece(h, half), ring_send.at[n], ring_recv.at[n], head=to * 2 + core)

    def swap(n, h, half):
        return remote(piece(h, half), piece(h, half), core_send.at[n], core_recv.at[n], head=y * 2 + 1 - core)

    ring(0, head, None, up).start()
    ring(1, head, None, down).start()
    swap(0, head, None).start()

    lax.fori_loop(B_DEV // 2, B_DEV * 3 // 4, prefix, 0)

    from_down, from_up, from_far = down * 2 + core, up * 2 + core, far * 2 + core
    ring(0, from_down, None, up).wait()
    ring(2, from_down, 0, up).start()
    swap(1, from_down, None).start()
    ring(1, from_up, None, down).wait()
    ring(3, from_up, 1, down).start()
    swap(2, from_up, None).start()

    lax.fori_loop(B_DEV * 3 // 4, B_DEV, prefix, 0)

    ring(2, from_far, 0, up).wait()
    swap(3, from_far, 0).start()
    ring(3, from_far, 1, down).wait()
    swap(4, from_far, 1).start()
    other = 1 - core
    swap(0, y * 2 + other, None).wait()
    swap(1, down * 2 + other, None).wait()
    swap(2, up * 2 + other, None).wait()
    swap(3, far * 2 + other, 0).wait()
    swap(4, far * 2 + other, 1).wait()

    def gather(p, _):
        for yy in range(NY):
            fork[p, yy * 144:yy * 144 + 80] = parts[2 * yy, p]
            fork[p, yy * 144 + 80:yy * 144 + 144] = parts[2 * yy + 1, p, 16:80]
        return 0

    lax.fori_loop(0, PAIRS, gather, 0)

    def forked(p, _):
        rows = pl.ds(pl.multiple_of(p * 128, 128), 128)
        keys = fork[p]
        s = dot(query(rows), keys[:LAT]) + dot(qr[rows, :], keys[LAT:])
        s = s * SCALE
        old = peak[rows, :][:, :1]
        m = jnp.maximum(jnp.max(s, axis=1, keepdims=True), old)
        w = jnp.exp(s - m).astype(BF)
        back = jnp.exp(old - m)
        norm = total[rows, :][:, :1] * back + jnp.sum(w.astype(F32), axis=1, keepdims=True)
        c = dot_nt(w, keys[:LAT])
        scale = 1.0 / norm
        for j in range(LANES):
            both = (ctx[j, rows, :] * back + c[:, j * 128:(j + 1) * 128]) * scale
            ctx[j, rows, :] = both.astype(BF).astype(F32)
        return 0

    lax.fori_loop(0, PAIRS, forked, 0)
    loads[6].wait()
    for h in range(HEADS):
        c = [ctx[j, pl.ds(h, ROWS, stride=HEADS), :] for j in range(LANES)]
        c = jnp.concatenate(c, axis=1).astype(BF)
        att[:, h * VDIM:(h + 1) * VDIM] = dot(c, vu[h]).astype(BF)


def project_kernel(
    att, wt, out,
    held, made, landed, cut, final,
    z_send, z_recv, r_send, r_recv, x_send, x_recv,
):
    me = lax.axis_index("branch")
    head = lax.axis_index("head")
    z, x = me // NX, lax.rem(me, NX)
    nxt = lax.rem(z + 1, NZ) * NX + x
    prv = lax.rem(z + NZ - 1, NZ) * NX + x

    barrier = pltpu.get_barrier_semaphore()
    for other in (nxt, prv):
        pl.semaphore_signal(barrier, inc=1, device_id={"branch": other}, device_id_type=MESH)
    for i in range(1, NX):
        pl.semaphore_signal(barrier, inc=1, device_id={"branch": z * NX + lax.rem(x + i, NX)}, device_id_type=MESH)
    for i in range(1, 8):
        pl.semaphore_signal(barrier, inc=1, device_id={"head": lax.rem(head + i, 8)}, device_id_type=MESH)
    pl.semaphore_wait(barrier, 2 + 3 + 7)

    def half(slot, s):
        if slot == 0:
            return att.at[pl.ds(s * HALF, HALF)]
        return held.at[slot, pl.ds(s * HALF, HALF)]

    def hop(way, k, s):
        came, goes = (k - 1, k) if way == 0 else ((9 - k) % 8, 8 - k)
        return remote(
            half(came, s), half(goes, s), z_send.at[way, k - 1, s], z_recv.at[way, k - 1, s],
            branch=nxt if way == 0 else prv,
        )

    hops = []

    def go(way, k, s):
        c = hop(way, k, s)
        c.start()
        hops.append(c)

    def reduce_copy(slot):
        return remote(made.at[slot], landed.at[head], r_send.at[slot], r_recv.at[head], head=lax.rem(z + 8 - slot, 8))

    def multiply(slot):
        a = att[...] if slot == 0 else held[slot]
        made[slot] = dot_nt(a, wt[...]).astype(BF)

        @pl.when(lax.rem(z + 8 - slot, 8) != head)
        def _():
            reduce_copy(slot).start()

    for s in (0, 1):
        go(0, 1, s)
        go(1, 1, s)
    multiply(0)
    for k in (1, 2, 3):
        for s in (0, 1):
            for way in (0, 1):
                t = s if way == 0 else 1 - s
                hop(way, k, t).wait_recv()
                if k < 3 or t == way:
                    go(way, k + 1, t)
        multiply(k)
        multiply(8 - k)
    hop(0, 4, 0).wait_recv()
    hop(1, 4, 1).wait_recv()
    multiply(4)

    acc = made[lax.rem(z + 8 - head, 8)].astype(F32)
    for i in range(1, 8):
        src = lax.rem(head + i, 8)
        remote(made.at[0], landed.at[src], r_send.at[0], r_recv.at[src], head=src).wait_recv()
        acc = acc + landed[src].astype(F32)
    acc = acc.astype(BF)
    for i in range(NX):
        cut[i] = acc[:, i * COLS:(i + 1) * COLS]
    final[x] = cut[x]
    spread = []
    for i in range(1, NX):
        d = lax.rem(x + i, NX)
        c = remote(cut.at[d], final.at[x], x_send.at[i], x_recv.at[x], branch=z * NX + d)
        c.start()
        spread.append(c)
    for i in range(1, NX):
        d = lax.rem(x + i, NX)
        remote(cut.at[d], final.at[d], x_send.at[i], x_recv.at[d], branch=z * NX + d).wait_recv()
    for i in range(NX):
        out[i * ROWS:(i + 1) * ROWS, :] = final[i]

    for c in hops:
        c.wait_send()
    for c in spread:
        c.wait_send()
    for slot in range(8):

        @pl.when(lax.rem(z + 8 - slot, 8) != head)
        def _(slot=slot):
            reduce_copy(slot).wait_send()


def attend(parent, lengths, table, qn, qr, ku, vu, pool, recent, nl):
    any_spec = pl.BlockSpec(memory_space=pl.ANY)
    smem = pl.BlockSpec(memory_space=pltpu.SMEM)
    dma = pltpu.SemaphoreType.DMA
    return pl.pallas_call(
        attend_kernel,
        out_shape=jax.ShapeDtypeStruct((ROWS, HEADS * VDIM), BF),
        in_specs=[smem] * 3 + [any_spec] * 7,
        out_specs=pl.BlockSpec(memory_space=pltpu.VMEM),
        scratch_shapes=[
            pltpu.VMEM((ROWS, HEADS * NOPE), BF),
            pltpu.VMEM((QROWS, ROPE), BF),
            pltpu.VMEM((HEADS, NOPE, LAT), BF),
            pltpu.VMEM((HEADS, LAT, VDIM), BF),
            pltpu.VMEM((B_DEV, WIDTH, BLOCK), BF),
            pltpu.VMEM((ROWS, WIDTH), BF),
            pltpu.VMEM((WIDTH, 128), BF),
            pltpu.VMEM((LANES, QROWS, 128), F32),
            pltpu.VMEM((LANES, QROWS, 128), F32),
            pltpu.VMEM((QROWS, 128), F32),
            pltpu.VMEM((QROWS, 128), F32),
            pltpu.VMEM((B_DEV, PART, 128), BF),
            pltpu.VMEM((GROUPS, PART, 128), BF),
            pltpu.VMEM((GROUPS, PART, 128), BF),
            pltpu.VMEM((1, 128), jnp.int32),
            pltpu.VMEM((GROUPS, 1, 128), jnp.int32),
            pltpu.VMEM((GROUPS, 1, 128), jnp.int32),
            pltpu.SMEM((GROUPS, 1, 128), jnp.int32),
            pltpu.VMEM((8, PAIRS, PART, 128), BF),
            pltpu.VMEM((PAIRS, WIDTH, BLOCK), BF),
            dma((7,)), dma,
            dma((GROUPS,)), dma((GROUPS,)), dma((GROUPS,)), dma((GROUPS,)),
            dma((4,)), dma((4,)), dma((5,)), dma((5,)),
        ],
        compiler_params=pltpu.CompilerParams(
            collective_id=0, has_side_effects=True, vmem_limit_bytes=48 * 2**20
        ),
        cost_estimate=pl.CostEstimate(flops=1_300_000_000, bytes_accessed=12_000_000, transcendentals=400_000),
    )(parent, lengths, table, qn, qr, ku, vu, pool, recent, nl)


def project(att, wt):
    vmem = pl.BlockSpec(memory_space=pltpu.VMEM)
    dma = pltpu.SemaphoreType.DMA
    return pl.pallas_call(
        project_kernel,
        out_shape=jax.ShapeDtypeStruct((NX * ROWS, COLS), BF),
        in_specs=[vmem, vmem],
        out_specs=vmem,
        scratch_shapes=[
            pltpu.VMEM((8, ROWS, HEADS * VDIM), BF),
            pltpu.VMEM((8, ROWS, NX * COLS), BF),
            pltpu.VMEM((8, ROWS, NX * COLS), BF),
            pltpu.VMEM((NX, ROWS, COLS), BF),
            pltpu.VMEM((NX, ROWS, COLS), BF),
            dma((2, 4, 2)), dma((2, 4, 2)), dma((8,)), dma((8,)), dma((NX,)), dma((NX,)),
        ],
        compiler_params=pltpu.CompilerParams(
            collective_id=1, has_side_effects=True, vmem_limit_bytes=48 * 2**20
        ),
        cost_estimate=pl.CostEstimate(flops=2_900_000_000, bytes_accessed=6_000_000, transcendentals=0),
    )(att, wt)


def local(
    query_nope, query_rope, key_up, value_up, out_weight, block_pool, recent_blocks, new_latent,
    parent, lengths, block_table,
):
    groups = [[zz * NX + xx for xx in range(NX)] for zz in range(NZ)]
    wt = lax.all_gather(out_weight.T, "branch", axis=0, tiled=True, axis_index_groups=groups)
    att = attend(
        parent, lengths, block_table.reshape(B_DEV), query_nope, query_rope.reshape(QROWS, ROPE), key_up, value_up,
        jnp.swapaxes(block_pool, 1, 2), jnp.swapaxes(recent_blocks, 1, 2), new_latent,
    )
    return project(att, wt)


def solution(mesh):
    return jax.shard_map(
        local,
        mesh=mesh,
        in_specs=(
            P("branch", "head"),
            P("branch", "head"),
            P("head", None, None),
            P("head", None, None),
            P("head", "branch"),
            P("branch", None, None),
            P("branch", None, None),
            P("branch", None),
            P("branch"),
            P("branch"),
            P("branch", None),
        ),
        out_specs=P("head", "branch"),
        check_vma=False,
    )
```

time: 449 us -> 136 us (0.30)
  waiting for transfers between devices: 336 us -> 0.73 us
  Pallas kernels: 0 us -> 109 us
  matrix products: 27 us -> 0 us
  blocking collectives: 22.5 us -> 0 us
  local copies, waits for them, and re-layouts: 30.1 us -> 11.1 us
  other arithmetic: 7.27 us -> 0 us
  starting transfers between devices: 6.53 us -> 0.01 us
    all_to_all x1 -> x0, waiting for transfers between devices: 185 us -> none  [local(): lax.all_to_all(outgoing, 'branch', split_axis=0, concat_axis=0, tiled=True)]
    all_gather x1, waiting for transfers between devices: 120 us -> 0.02 us  [local(): lax.all_gather(out_weight.T, 'branch', axis=0, tiled=True, axis_index_gro...]
    pallas_call x0 -> x2, Pallas kernels: none -> 109 us  [the longest x1 54.6 us: attend(): pl.pallas_call(attend_kernel, out_shape=jax.ShapeDtypeStruct((ROWS, HEADS...]
    reduce_scatter x1 -> x0, waiting for transfers between devices: 31.1 us -> none  [local(): lax.psum_scatter(partial_rows, 'head', scatter_dimension=0, tiled=True)]
    dot_general x9 -> x0, matrix products: 27 us -> none  [the longest x1 10.4 us: local(): jnp.dot(lax.all_gather(attended, 'branch', axis=0, tiled=True), out_weigh...]
    unnamed x1 -> x0, blocking collectives: 22.5 us -> none
    gather x3 -> x0, local copies, waits for them, and re-layouts: 15.8 us -> none  [the longest x1 6.62 us: local(): forked_rows = incoming[source, own_rank]]
    all_to_all x1 -> x0, starting transfers between devices: 6.05 us -> none  [local(): lax.all_to_all(outgoing, 'branch', split_axis=0, concat_axis=0, tiled=True)]
  transfers between devices with their start and end apart: 3 -> 1, of which waited for: 3 -> 0; matrix products, arithmetic and copies ran while one was open for 3% -> 1% of each run, Pallas kernels for 0% -> 41%
where the time goes in v1:
time: 136 us; the launch traced here: 135 us
  Pallas kernels  109 us (80%)
  between operations  13.4 us (10%)
  local copies, waits for them, and re-layouts  11.1 us (8%)
    pallas_call x1, Pallas kernels, attend(): pl.pallas_call(attend_kernel, out_shape=jax.ShapeDtypeStruct((ROWS, HEADS...  54.6 us
    pallas_call x1, Pallas kernels, project(): pl.pallas_call(project_kernel, out_shape=jax.ShapeDtypeStruct((NX * ROWS,...  54.6 us
    unnamed x16, local copies, waits for them, and re-layouts  9.07 us
  transfers between devices with their start and end apart: 1, of which 0 were waited for; matrix products, arithmetic and copies ran while one was open for 1% of the time, Pallas kernels for 41%

profile of v1, /device:TPU:18, one launch (start us, length us, event | category | flops | bytes accessed | tf_op | source)
XLA Modules:
  0.0 134.5 jit_solution(4101606036251668017)
XLA Ops:
  6.5 0.0 all-gather.2.cloned.1.call-start
  6.5 0.7 all-gather.2.cloned.1.call-update
  7.3 1.2 reshape.7.qr_hbm
  8.5 0.0 copy-start
  8.5 1.6 %copy-done = bf16[16,128,512]{2,1,0:T(8,128)(2,1)S(1)} copy-done((bf16[16,128,512]{2,1,0:T(8,128)(2,1)S(1)}, bf16[16,128,512]{2,1,0:T(8,128)(2,1)}, u32[]{:S(2)}) %copy-start) | copy-done | bytes 2097176
  10.1 0.0 copy-start.1
  10.1 1.6 %copy-done.1 = bf16[16,512,128]{2,1,0:T(8,128)(2,1)S(1)} copy-done((bf16[16,512,128]{2,1,0:T(8,128)(2,1)S(1)}, bf16[16,512,128]{2,1,0:T(8,128)(2,1)}, u32[]{:S(2)}) %copy-start.1) | copy-done | bytes 2097176
  11.7 0.0 copy-start.2
  11.7 1.0 copy-done.2
  12.7 0.0 copy-start.3
  12.7 0.9 copy-done.3
  13.6 0.0 copy-start.4
  13.6 0.7 copy-done.4
  14.2 0.0 copy-start.5
  14.2 0.7 copy-done.5
  14.9 0.0 copy-start.6
  14.9 0.7 copy-done.6
  15.5 54.6 %shard_map.109.att = bf16[96,2048]{1,0:T(8,128)(2,1)S(1)} custom-call(s32[24]{0:T(128)S(1)} %copy-done.4, s32[24]{0:T(128)S(1)} %copy-done.5, s32[24]{0:T(128)S(1)} %bitcast.4, bf16[96,2048]{1,0:T(8,128)(2,1)S(1)} %copy-done.2, bf16[1536,64]{1,0:T(8,128)(2,1)S(1)} %reshape.7.qr_hbm, bf16[16,128,512]{2,1,0:T(8,128)(2,1)S(1)} %copy-done, ...), custom_call_target="tpu_custom_call" | custom-call | flops 1300000000 | bytes 12000000 | tf_op jit(solution)/shard_map/pallas_call | solution.py:351
  70.2 0.0 all-gather.2.cloned.1.call-done.wt
  70.2 0.0 copy-start.7
  70.2 2.0 %copy-done.7 = bf16[896,2048]{1,0:T(8,128)(2,1)S(1)} copy-done((bf16[896,2048]{1,0:T(8,128)(2,1)S(1)}, bf16[896,2048]{1,0:T(8,128)(2,1)}, u32[]{:S(2)}) %copy-start.7) | copy-done | bytes 3670040
  72.3 54.6 %shard_map.110 = bf16[384,224]{1,0:T(8,128)(2,1)S(1)} custom-call(bf16[96,2048]{1,0:T(8,128)(2,1)S(1)} %shard_map.109.att, bf16[896,2048]{1,0:T(8,128)(2,1)S(1)} %copy-done.7), custom_call_target="tpu_custom_call" | custom-call | flops 2900000000 | bytes 6000000 | tf_op jit(solution)/shard_map/pallas_call | solution.py:391
  126.9 0.8 copy.13
Async XLA Ops:
  6.5 63.7 %all-gather.2.cloned.1.call-start = ((), (), s32[]{:S(2)}) async-start(), calls=%async_computation | async-start | bytes 4587520 | tf_op jit(solution)/shard_map/all_gather | solution.py:416
  8.5 1.6 %copy-start = (bf16[16,128,512]{2,1,0:T(8,128)(2,1)S(1)}, bf16[16,128,512]{2,1,0:T(8,128)(2,1)}, u32[]{:S(2)}) copy-start(bf16[16,128,512]{2,1,0:T(8,128)(2,1)} %ku_hbm.1) | copy-start | bytes 6291460
  10.1 1.6 %copy-start.1 = (bf16[16,512,128]{2,1,0:T(8,128)(2,1)S(1)}, bf16[16,512,128]{2,1,0:T(8,128)(2,1)}, u32[]{:S(2)}) copy-start(bf16[16,512,128]{2,1,0:T(8,128)(2,1)} %vu_hbm.1) | copy-start | bytes 6291460
  11.7 1.0 copy-start.2
  12.7 0.9 copy-start.3
  13.6 0.7 copy-start.4
  14.2 0.7 copy-start.5
  14.9 0.7 copy-start.6
  70.2 2.0 %copy-start.7 = (bf16[896,2048]{1,0:T(8,128)(2,1)S(1)}, bf16[896,2048]{1,0:T(8,128)(2,1)}, u32[]{:S(2)}) copy-start(bf16[896,2048]{1,0:T(8,128)(2,1)} %all-gather.2.cloned.1.call-done.wt) | copy-start | bytes 11010052
Sparse Core Ops, SparseCore 0:
  9.2 55.6 all-gather.1

commit v2 on v1

v2 whole, which is shorter than its diff:
```python
import functools

import jax
import jax.numpy as jnp
from jax import lax
from jax.experimental import pallas as pl
from jax.experimental.pallas import tpu as pltpu
from jax.sharding import PartitionSpec as P

NOPE = 128
ROPE = 64
LAT = 512
VDIM = 128
BLOCK = 128
STEPS = 4
B_DEV = 24
PAIRS = B_DEV // 2
WIDTH = LAT + ROPE
HEADS = 16
ROWS = B_DEV * STEPS
HALF = ROWS // 2
QROWS = ROWS * HEADS
COLS = 224
NZ, NX, NY = 8, 4, 4
GROUPS = NZ * NX
PART = 80
VMEM_BYTES = 60 * 2**20
LANES = LAT // 128
SCALE = (NOPE + ROPE) ** -0.5
BF = jnp.bfloat16
F32 = jnp.float32
MESH = pl.DeviceIdType.MESH
NT = (((1,), (1,)), ((), ()))


def dot(a, b):
    return jnp.dot(a, b, preferred_element_type=F32)


def dot_nt(a, b):
    return lax.dot_general(a, b, NT, preferred_element_type=F32)


def remote(src, dst, send, recv, **where):
    return pltpu.make_async_remote_copy(
        src_ref=src, dst_ref=dst, send_sem=send, recv_sem=recv,
        device_id=where, device_id_type=MESH,
    )


def layer_kernel(
    par_hbm, lens_hbm, table_hbm,
    qn_hbm, qr_hbm, ku_hbm, vu_hbm, pool_hbm, recent_hbm, nl_hbm, w_hbm,
    out,
    par, lens, table,
    qn, qr, ku, vu, pool, nl, nlt, wt,
    qs, ctx, peak, total,
    mine, packed, slots, my_par, all_par, pick_v, pick_s, parts, fork,
    held, made, landed, cut, final,
    load_sem, pick_sem, par_send, par_recv, out_send, out_recv, ring_send, ring_recv, core_send, core_recv,
    w_send, w_recv, z_send, z_recv, r_send, r_recv, x_send, x_recv,
):
    me = lax.axis_index("branch")
    head = lax.axis_index("head")
    z, x = me // NX, lax.rem(me, NX)
    y, core = head // 2, lax.rem(head, 2)
    up, down = lax.rem(y + 1, NY), lax.rem(y + 3, NY)
    far = lax.rem(y + 2, NY)
    left, right = lax.rem(x + 3, NX), lax.rem(x + 1, NX)
    nxt = lax.rem(z + 1, NZ) * NX + x
    prv = lax.rem(z + NZ - 1, NZ) * NX + x
    row0 = pl.multiple_of(y * 144 + core * 64, 16)

    def columns(i, start=0, size=COLS):
        return wt.at[pl.ds(pl.multiple_of(i * COLS + start, 16), size)]

    pairs = (
        (par_hbm, par), (recent_hbm.at[:, pl.ds(row0, PART), :], mine), (ku_hbm, ku), (qn_hbm, qn), (qr_hbm, qr),
        (lens_hbm, lens), (table_hbm, table), (pool_hbm, pool), (nl_hbm, nl), (vu_hbm, vu), (w_hbm, columns(x)),
    )
    loads = [pltpu.make_async_copy(src, dst, load_sem.at[i]) for i, (src, dst) in enumerate(pairs)]
    for load in loads:
        load.start()

    barrier = pltpu.get_barrier_semaphore()

    def greet(i, _):
        pl.semaphore_signal(barrier, inc=1, device_id={"branch": lax.rem(me + i, GROUPS)}, device_id_type=MESH)
        return 0

    lax.fori_loop(1, GROUPS, greet, 0)
    for i in range(1, 8):
        pl.semaphore_signal(barrier, inc=1, device_id={"head": lax.rem(head + i, 8)}, device_id_type=MESH)

    loads[0].wait()
    lane = lax.broadcasted_iota(jnp.int32, (1, 128), 1)
    row = jnp.zeros((1, 128), jnp.int32) - 1
    for b in range(0, B_DEV, 2):
        row = jnp.where(lane == b, par[b], row)
    my_par[...] = row
    all_par[me] = row
    pl.semaphore_wait(barrier, GROUPS - 1 + 7)

    def start_par(i, _):
        d = lax.rem(me + i, GROUPS)
        remote(my_par, all_par.at[me], par_send.at[i], par_recv.at[me], branch=d).start()
        return 0

    lax.fori_loop(1, GROUPS, start_par, 0)

    loads[2].wait()
    loads[3].wait()
    for h in range(HEADS):
        q = dot(qn[:, h * NOPE:(h + 1) * NOPE], ku[h]).astype(BF).astype(F32)
        for j in range(LANES):
            qs[j, pl.ds(h, ROWS, stride=HEADS), :] = q[:, j * 128:(j + 1) * 128]
    loads[4].wait()
    low = lax.broadcasted_iota(jnp.int32, (ROWS, 128), 1) < ROPE
    for h in range(HEADS):
        q = qr[:, (h // 2) * 128:(h // 2 + 1) * 128].astype(F32)
        qs[LANES, pl.ds(h, ROWS, stride=HEADS), :] = jnp.where(low if h % 2 == 0 else ~low, q, 0.0)

    def wait_par(i, _):
        src = lax.rem(me + i, GROUPS)
        remote(my_par, all_par.at[src], par_send.at[i], par_recv.at[src], branch=src).wait()
        return 0

    lax.fori_loop(1, GROUPS, wait_par, 0)
    local = all_par[...] - me * B_DEV
    hit = (local >= 0) & (local < B_DEV)
    pick_v[...] = jnp.broadcast_to(
        jnp.sum(jnp.where(hit, local, 0), axis=2, keepdims=True), (GROUPS, 1, 128)
    )
    pick = pltpu.make_async_copy(pick_v, pick_s, pick_sem)
    pick.start()
    loads[1].wait()
    pick.wait()

    def send_block(i, _):
        d = lax.rem(me + i, GROUPS)
        packed[d] = mine[pick_s[d, 0, 0]]
        remote(packed.at[d], slots.at[me], out_send.at[d], out_recv.at[me], branch=d).start()
        return 0

    lax.fori_loop(1, GROUPS, send_block, 0)
    slots[me] = mine[pick_s[me, 0, 0]]

    loads[10].wait()

    def share(n, owner, start, size, to):
        return remote(
            columns(owner, start, size), columns(owner, start, size), w_send.at[n], w_recv.at[n], branch=z * NX + to
        )

    share(0, x, 0, COLS, right).start()
    share(1, x, 0, COLS, left).start()

    for n in (5, 6, 7, 8):
        loads[n].wait()
    nlt[...] = jnp.zeros_like(nlt)
    nlt[:, :ROWS] = nl[...].astype(F32).T.astype(BF)

    key = lax.broadcasted_iota(jnp.int32, (STEPS * HEADS, 256), 1)
    step = lax.broadcasted_iota(jnp.int32, (STEPS * HEADS, 256), 0) // HEADS

    def query(rows):
        return jnp.concatenate([qs[j, rows, :] for j in range(LANES + 1)], axis=1).astype(BF)

    def scores(rows, keys):
        return dot(query(rows), jnp.concatenate([keys, keys[LAT:]], axis=0))

    def prefix(b, _):
        rows = pl.ds(pl.multiple_of(b * 64, 64), 64)
        keys = jnp.concatenate([pool[table[b]], nlt[...]], axis=1)
        s = scores(rows, keys)
        fresh = key - BLOCK - b * STEPS
        allowed = (key < lens[b]) | ((fresh >= 0) & (fresh <= step))
        s = jnp.where(allowed, s * SCALE, -jnp.inf)
        m = jnp.max(s, axis=1, keepdims=True)
        w = jnp.exp(s - m).astype(BF)
        total[rows, :] = jnp.broadcast_to(jnp.sum(w.astype(F32), axis=1, keepdims=True), (64, 128))
        peak[rows, :] = jnp.broadcast_to(m, (64, 128))
        c = dot_nt(w, keys[:LAT])
        for j in range(LANES):
            ctx[j, rows, :] = c[:, j * 128:(j + 1) * 128]
        return 0

    lax.fori_loop(0, B_DEV // 2, prefix, 0)

    def wait_block(i, _):
        src = lax.rem(me + i, GROUPS)
        remote(packed.at[src], slots.at[src], out_send.at[src], out_recv.at[src], branch=src).wait()
        return 0

    lax.fori_loop(1, GROUPS, wait_block, 0)
    for p in range(PAIRS):
        parts[head, p] = slots[par[2 * p] // B_DEV]

    def piece(h, half):
        at = parts.at[h]
        return at if half is None else at.at[pl.ds(half * (PAIRS // 2), PAIRS // 2)]

    def ring(n, h, half, to):
        return remote(piece(h, half), piece(h, half), ring_send.at[n], ring_recv.at[n], head=to * 2 + core)

    def swap(n, h, half):
        return remote(piece(h, half), piece(h, half), core_send.at[n], core_recv.at[n], head=y * 2 + 1 - core)

    ring(0, head, None, up).start()
    ring(1, head, None, down).start()
    swap(0, head, None).start()

    lax.fori_loop(B_DEV // 2, B_DEV * 3 // 4, prefix, 0)

    from_down, from_up, from_far = down * 2 + core, up * 2 + core, far * 2 + core
    ring(0, from_down, None, up).wait()
    ring(2, from_down, 0, up).start()
    swap(1, from_down, None).start()
    ring(1, from_up, None, down).wait()
    ring(3, from_up, 1, down).start()
    swap(2, from_up, None).start()

    lax.fori_loop(B_DEV * 3 // 4, B_DEV, prefix, 0)

    share(0, left, 0, COLS, right).wait()
    share(2, left, 0, COLS // 2, right).start()
    share(1, right, 0, COLS, left).wait()
    share(3, right, COLS // 2, COLS // 2, left).start()

    ring(2, from_far, 0, up).wait()
    swap(3, from_far, 0).start()
    ring(3, from_far, 1, down).wait()
    swap(4, from_far, 1).start()
    other = 1 - core
    swap(0, y * 2 + other, None).wait()
    swap(1, down * 2 + other, None).wait()
    swap(2, up * 2 + other, None).wait()
    swap(3, far * 2 + other, 0).wait()
    swap(4, far * 2 + other, 1).wait()

    def gather(p, _):
        for yy in range(NY):
            fork[p, yy * 144:yy * 144 + 80] = parts[2 * yy, p]
            fork[p, yy * 144 + 80:yy * 144 + 144] = parts[2 * yy + 1, p, 16:80]
        return 0

    lax.fori_loop(0, PAIRS, gather, 0)

    def forked(p, _):
        rows = pl.ds(pl.multiple_of(p * 128, 128), 128)
        keys = fork[p]
        s = scores(rows, keys) * SCALE
        old = peak[rows, :][:, :1]
        m = jnp.maximum(jnp.max(s, axis=1, keepdims=True), old)
        w = jnp.exp(s - m).astype(BF)
        back = jnp.exp(old - m)
        norm = total[rows, :][:, :1] * back + jnp.sum(w.astype(F32), axis=1, keepdims=True)
        c = dot_nt(w, keys[:LAT])
        scale = 1.0 / norm
        for j in range(LANES):
            both = (ctx[j, rows, :] * back + c[:, j * 128:(j + 1) * 128]) * scale
            ctx[j, rows, :] = both.astype(BF).astype(F32)
        return 0

    def half_of(slot, s):
        return held.at[slot, pl.ds(s * HALF, HALF)]

    def hop(way, k, s):
        came, goes = (k - 1, k) if way == 0 else ((9 - k) % 8, 8 - k)
        return remote(
            half_of(came, s), half_of(goes, s), z_send.at[way, k - 1, s], z_recv.at[way, k - 1, s],
            branch=nxt if way == 0 else prv,
        )

    hops = []

    def go(way, k, s):
        c = hop(way, k, s)
        c.start()
        hops.append(c)

    loads[9].wait()
    for s in (0, 1):
        lax.fori_loop(s * (PAIRS // 2), (s + 1) * (PAIRS // 2), forked, 0)
        for h in range(HEADS):
            c = [ctx[j, pl.ds(s * HALF * HEADS + h, HALF, stride=HEADS), :] for j in range(LANES)]
            c = jnp.concatenate(c, axis=1).astype(BF)
            held[0, s * HALF:(s + 1) * HALF, h * VDIM:(h + 1) * VDIM] = dot(c, vu[h]).astype(BF)
        go(0, 1, s)
        go(1, 1, s)

    share(2, lax.rem(x + 2, NX), 0, COLS // 2, right).wait()
    share(3, lax.rem(x + 2, NX), COLS // 2, COLS // 2, left).wait()

    def reduce_copy(slot):
        return remote(made.at[slot], landed.at[head], r_send.at[slot], r_recv.at[head], head=lax.rem(z + 8 - slot, 8))

    def multiply(slot):
        made[slot] = dot_nt(held[slot], wt[...]).astype(BF)

        @pl.when(lax.rem(z + 8 - slot, 8) != head)
        def _():
            reduce_copy(slot).start()

    multiply(0)
    for k in (1, 2, 3):
        for s in (0, 1):
            for way in (0, 1):
                t = s if way == 0 else 1 - s
                hop(way, k, t).wait_recv()
                if k < 3 or t == way:
                    go(way, k + 1, t)
            if s == 0 and k > 1:
                multiply(9 - k)
        multiply(k)
    multiply(5)
    hop(0, 4, 0).wait_recv()
    hop(1, 4, 1).wait_recv()
    multiply(4)

    acc = made[lax.rem(z + 8 - head, 8)].astype(F32)
    for i in range(1, 8):
        src = lax.rem(head + i, 8)
        remote(made.at[0], landed.at[src], r_send.at[0], r_recv.at[src], head=src).wait_recv()
        acc = acc + landed[src].astype(F32)
    acc = acc.astype(BF)
    for i in range(NX):
        cut[i] = acc[:, i * COLS:(i + 1) * COLS]
    final[x] = cut[x]
    spread = []
    for i in range(1, NX):
        d = lax.rem(x + i, NX)
        c = remote(cut.at[d], final.at[x], x_send.at[i], x_recv.at[x], branch=z * NX + d)
        c.start()
        spread.append(c)
    for i in range(1, NX):
        d = lax.rem(x + i, NX)
        remote(cut.at[d], final.at[d], x_send.at[i], x_recv.at[d], branch=z * NX + d).wait_recv()
    for i in range(NX):
        out[i * ROWS:(i + 1) * ROWS, :] = final[i]

    for c in hops:
        c.wait_send()
    for c in spread:
        c.wait_send()
    for slot in range(8):

        @pl.when(lax.rem(z + 8 - slot, 8) != head)
        def _(slot=slot):
            reduce_copy(slot).wait_send()


def layer(*operands):
    vmem, dma = pltpu.VMEM, pltpu.SemaphoreType.DMA
    smem = pltpu.SMEM
    return pl.pallas_call(
        layer_kernel,
        out_shape=jax.ShapeDtypeStruct((NX * ROWS, COLS), BF),
        in_specs=[pl.BlockSpec(memory_space=pl.ANY)] * 11,
        out_specs=pl.BlockSpec(memory_space=pltpu.VMEM),
        scratch_shapes=[
            smem((B_DEV,), jnp.int32), smem((B_DEV,), jnp.int32), smem((B_DEV,), jnp.int32),
            vmem((ROWS, HEADS * NOPE), BF),
            vmem((ROWS, HEADS * ROPE), BF),
            vmem((HEADS, NOPE, LAT), BF),
            vmem((HEADS, LAT, VDIM), BF),
            vmem((B_DEV, WIDTH, BLOCK), BF),
            vmem((ROWS, WIDTH), BF),
            vmem((WIDTH, 128), BF),
            vmem((NX * COLS, HEADS * VDIM), BF),
            vmem((LANES + 1, QROWS, 128), F32),
            vmem((LANES, QROWS, 128), F32),
            vmem((QROWS, 128), F32),
            vmem((QROWS, 128), F32),
            vmem((B_DEV, PART, 128), BF),
            vmem((GROUPS, PART, 128), BF),
            vmem((GROUPS, PART, 128), BF),
            vmem((1, 128), jnp.int32),
            vmem((GROUPS, 1, 128), jnp.int32),
            vmem((GROUPS, 1, 128), jnp.int32),
            smem((GROUPS, 1, 128), jnp.int32),
            vmem((8, PAIRS, PART, 128), BF),
            vmem((PAIRS, WIDTH, BLOCK), BF),
            vmem((8, ROWS, HEADS * VDIM), BF),
            vmem((8, ROWS, NX * COLS), BF),
            vmem((8, ROWS, NX * COLS), BF),
            vmem((NX, ROWS, COLS), BF),
            vmem((NX, ROWS, COLS), BF),
            dma((11,)), dma,
            dma((GROUPS,)), dma((GROUPS,)), dma((GROUPS,)), dma((GROUPS,)),
            dma((4,)), dma((4,)), dma((5,)), dma((5,)),
            dma((4,)), dma((4,)), dma((2, 4, 2)), dma((2, 4, 2)), dma((8,)), dma((8,)), dma((NX,)), dma((NX,)),
        ],
        compiler_params=pltpu.CompilerParams(
            collective_id=0, has_side_effects=True, vmem_limit_bytes=VMEM_BYTES
        ),
        cost_estimate=pl.CostEstimate(flops=4_200_000_000, bytes_accessed=16_000_000, transcendentals=400_000),
    )(*operands)


def local(
    query_nope, query_rope, key_up, value_up, out_weight, block_pool, recent_blocks, new_latent,
    parent, lengths, block_table,
):
    return layer(
        parent, lengths, block_table.reshape(B_DEV), query_nope, query_rope, key_up, value_up,
        jnp.swapaxes(block_pool, 1, 2), jnp.swapaxes(recent_blocks, 1, 2), new_latent, out_weight.T,
    )


def solution(mesh):
    return jax.shard_map(
        local,
        mesh=mesh,
        in_specs=(
            P("branch", "head"),
            P("branch", "head"),
            P("head", None, None),
            P("head", None, None),
            P("head", "branch"),
            P("branch", None, None),
            P("branch", None, None),
            P("branch", None),
            P("branch"),
            P("branch"),
            P("branch", None),
        ),
        out_specs=P("head", "branch"),
        check_vma=False,
    )
```

time: 136 us -> 106 us (0.78)
  between operations: 13.4 us -> 0.01 us
  local copies, waits for them, and re-layouts: 11.1 us -> 1.73 us
  Pallas kernels: 109 us -> 103 us
    unnamed x16 -> x0, local copies, waits for them, and re-layouts: 9.07 us -> none
    pallas_call x2 -> x1, Pallas kernels: 109 us -> 103 us  [layer(): pl.pallas_call(layer_kernel, out_shape=jax.ShapeDtypeStruct((NX * ROWS, C...]
  transfers between devices with their start and end apart: 1 -> 0, of which waited for: 0 -> 0; matrix products, arithmetic and copies ran while one was open for 1% -> 0% of each run, Pallas kernels for 41% -> 0%
where the time goes in v2:
time: 106 us; the launch traced here: 105 us
  Pallas kernels  103 us (97%)
  local copies, waits for them, and re-layouts  1.73 us (2%)
    pallas_call x1, Pallas kernels, layer(): pl.pallas_call(layer_kernel, out_shape=jax.ShapeDtypeStruct((NX * ROWS, C...  103 us

profile of v2, /device:TPU:18, one launch (start us, length us, event | category | flops | bytes accessed | tf_op | source)
XLA Modules:
  0.0 105.1 jit_solution(7929860728783854747)
XLA Ops:
  0.0 103.4 %shard_map.109 = bf16[384,224]{1,0:T(8,128)(2,1)} custom-call(s32[24]{0:T(128)} %par_hbm.1, s32[24]{0:T(128)} %lens_hbm.1, s32[24]{0:T(128)} %bitcast.7, bf16[96,2048]{1,0:T(8,128)(2,1)} %qn_hbm.1, bf16[96,1024]{1,0:T(8,128)(2,1)} %qr_hbm.1, bf16[16,128,512]{2,1,0:T(8,128)(2,1)} %ku_hbm.1, bf16[16,512,128]{2,1,0:T(8,128)(2,1)} %vu_hbm.1, ...), custom_call_target="tpu_custom_call" | custom-call | flops 4200000000 | bytes 16000000 | tf_op jit(solution)/shard_map/pallas_call | solution.py:356
  103.4 1.7 %copy.12 = bf16[384,224]{0,1:T(8,128)(2,1)} copy(bf16[384,224]{1,0:T(8,128)(2,1)} %shard_map.109) | data formatting | bytes 344064 | tf_op jit(solution)/shard_map/pallas_call | solution.py:356

commit v3 on v2

--- a/solution.py
+++ b/solution.py
@@ -23,14 +23,21 @@
 COLS = 224
 NZ, NX, NY = 8, 4, 4
 GROUPS = NZ * NX
-PART = 80
+PART_A, PART_B = 48, 32
+PART = PART_A + PART_B
+SLICE = COLS // 2
 VMEM_BYTES = 60 * 2**20
 LANES = LAT // 128
+TOGETHER = 3
+LAG = 2
 SCALE = (NOPE + ROPE) ** -0.5
 BF = jnp.bfloat16
 F32 = jnp.float32
 MESH = pl.DeviceIdType.MESH
 NT = (((1,), (1,)), ((), ()))
+
+
+SIZES = (32, 16)
 
 
 def dot(a, b):
@@ -55,10 +62,10 @@
     par, lens, table,
     qn, qr, ku, vu, pool, nl, nlt, wt,
     qs, ctx, peak, total,
-    mine, packed, slots, my_par, all_par, pick_v, pick_s, parts, fork,
-    held, made, landed, cut, final,
+    mine, packed, slots_a, slots_b, my_par, all_par, pick_v, pick_s, parts_a, parts_b,
+    held, made, landed, done, final,
     load_sem, pick_sem, par_send, par_recv, out_send, out_recv, ring_send, ring_recv, core_send, core_recv,
-    w_send, w_recv, z_send, z_recv, r_send, r_recv, x_send, x_recv,
+    w_send, w_recv, z_send, z_recv, r_send, r_recv, f_send, f_recv,
 ):
     me = lax.axis_index("branch")
     head = lax.axis_index("head")
@@ -69,19 +76,32 @@
     left, right = lax.rem(x + 3, NX), lax.rem(x + 1, NX)
     nxt = lax.rem(z + 1, NZ) * NX + x
     prv = lax.rem(z + NZ - 1, NZ) * NX + x
-    row0 = pl.multiple_of(y * 144 + core * 64, 16)
+    row0 = pl.multiple_of(y * 144 + core * PART, 16)
 
     def columns(i, start=0, size=COLS):
         return wt.at[pl.ds(pl.multiple_of(i * COLS + start, 16), size)]
 
     pairs = (
-        (par_hbm, par), (recent_hbm.at[:, pl.ds(row0, PART), :], mine), (ku_hbm, ku), (qn_hbm, qn), (qr_hbm, qr),
+        (par_hbm, par), (recent_hbm.at[:, pl.ds(row0, 64), :], mine.at[:, pl.ds(0, 64), :]), (ku_hbm, ku), (qn_hbm, qn), (qr_hbm, qr),
         (lens_hbm, lens), (table_hbm, table), (pool_hbm, pool), (nl_hbm, nl), (vu_hbm, vu), (w_hbm, columns(x)),
     )
     loads = [pltpu.make_async_copy(src, dst, load_sem.at[i]) for i, (src, dst) in enumerate(pairs)]
     for load in loads:
         load.start()
 
+    def extra():
+        return pltpu.make_async_copy(
+            recent_hbm.at[:, pl.ds(pl.multiple_of(y * 144 + 64, 16), 16), :], mine.at[:, pl.ds(64, 16), :], load_sem.at[11]
+        )
+
+    @pl.when(core == 0)
+    def _():
+        extra().start()
+
+    @pl.when(core == 1)
+    def _():
+        mine[:, 64:, :] = jnp.zeros((B_DEV, 16, 128), BF)
+
     barrier = pltpu.get_barrier_semaphore()
 
     def greet(i, _):
@@ -91,6 +111,14 @@
     lax.fori_loop(1, GROUPS, greet, 0)
     for i in range(1, 8):
         pl.semaphore_signal(barrier, inc=1, device_id={"head": lax.rem(head + i, 8)}, device_id_type=MESH)
+    for i in range(NX):
+        for n in range(2):
+
+            @pl.when((i != x) | (2 * x + n != head))
+            def _(i=i, n=n):
+                pl.semaphore_signal(
+                    barrier, inc=1, device_id={"branch": z * NX + i, "head": 2 * x + n}, device_id_type=MESH
+                )
 
     loads[0].wait()
     lane = lax.broadcasted_iota(jnp.int32, (1, 128), 1)
@@ -99,7 +127,7 @@
         row = jnp.where(lane == b, par[b], row)
     my_par[...] = row
     all_par[me] = row
-    pl.semaphore_wait(barrier, GROUPS - 1 + 7)
+    pl.semaphore_wait(barrier, GROUPS - 1 + 7 + jnp.where(y == x, 7, 8))
 
     def start_par(i, _):
         d = lax.rem(me + i, GROUPS)
@@ -134,16 +162,44 @@
     pick = pltpu.make_async_copy(pick_v, pick_s, pick_sem)
     pick.start()
     loads[1].wait()
+
+    @pl.when(core == 0)
+    def _():
+        extra().wait()
+
     pick.wait()
 
-    def send_block(i, _):
+    def block_a(n, at, to):
+        return remote(packed.at[n, pl.ds(0, PART_A)], slots_a.at[at], out_send.at[0, n], out_recv.at[0, at], branch=to)
+
+    def block_b(n, at, to, size):
+        return remote(
+            packed.at[n, pl.ds(PART_A, size)], slots_b.at[at, pl.ds(0, size)],
+            out_send.at[1, n], out_recv.at[1, at], branch=to,
+        )
+
+    def send_a(i, _):
         d = lax.rem(me + i, GROUPS)
         packed[d] = mine[pick_s[d, 0, 0]]
-        remote(packed.at[d], slots.at[me], out_send.at[d], out_recv.at[me], branch=d).start()
-        return 0
-
-    lax.fori_loop(1, GROUPS, send_block, 0)
-    slots[me] = mine[pick_s[me, 0, 0]]
+        block_a(d, me, d).start()
+        return 0
+
+    lax.fori_loop(1, GROUPS, send_a, 0)
+
+    for c in range(2):
+
+        @pl.when(core == c)
+        def _(c=c):
+            def send_b(i, _):
+                d = lax.rem(me + i, GROUPS)
+                block_b(d, me, d, SIZES[c]).start()
+                return 0
+
+            lax.fori_loop(1, GROUPS, send_b, 0)
+
+    own = mine[pick_s[me, 0, 0]]
+    slots_a[me] = own[:PART_A]
+    slots_b[me] = own[PART_A:]
 
     loads[10].wait()
 
@@ -187,79 +243,116 @@
 
     lax.fori_loop(0, B_DEV // 2, prefix, 0)
 
-    def wait_block(i, _):
+    def wait_a(i, _):
         src = lax.rem(me + i, GROUPS)
-        remote(packed.at[src], slots.at[src], out_send.at[src], out_recv.at[src], branch=src).wait()
-        return 0
-
-    lax.fori_loop(1, GROUPS, wait_block, 0)
+        block_a(src, src, src).wait()
+        return 0
+
+    lax.fori_loop(1, GROUPS, wait_a, 0)
     for p in range(PAIRS):
-        parts[head, p] = slots[par[2 * p] // B_DEV]
-
-    def piece(h, half):
-        at = parts.at[h]
+        parts_a[head, p] = slots_a[par[2 * p] // B_DEV]
+
+    from_down, from_up, from_far = down * 2 + core, up * 2 + core, far * 2 + core
+    other = 1 - core
+
+    def piece(h, part, size, half):
+        at = parts_a.at[h] if part == 0 else parts_b.at[h, :, pl.ds(0, size)]
         return at if half is None else at.at[pl.ds(half * (PAIRS // 2), PAIRS // 2)]
 
-    def ring(n, h, half, to):
-        return remote(piece(h, half), piece(h, half), ring_send.at[n], ring_recv.at[n], head=to * 2 + core)
-
-    def swap(n, h, half):
-        return remote(piece(h, half), piece(h, half), core_send.at[n], core_recv.at[n], head=y * 2 + 1 - core)
-
-    ring(0, head, None, up).start()
-    ring(1, head, None, down).start()
-    swap(0, head, None).start()
-
+    def ring(n, h, part, size, half, to):
+        at = piece(h, part, size, half)
+        return remote(at, at, ring_send.at[part, n], ring_recv.at[part, n], head=to * 2 + core)
+
+    def swap(n, h, part, size, half):
+        at = piece(h, part, size, half)
+        return remote(at, at, core_send.at[part, n], core_recv.at[part, n], head=y * 2 + other)
+
+    def ring_first(part, size):
+        ring(0, head, part, size, None, up).start()
+        ring(1, head, part, size, None, down).start()
+        swap(0, head, part, size, None).start()
+
+    def ring_second(part, size):
+        ring(0, from_down, part, size, None, up).wait()
+        ring(2, from_down, part, size, 0, up).start()
+        ring(1, from_up, part, size, None, down).wait()
+        ring(3, from_up, part, size, 1, down).start()
+        swap(1, from_down, part, size, None).start()
+        swap(2, from_up, part, size, None).start()
+
+    def ring_third(part, size):
+        ring(2, from_far, part, size, 0, up).wait()
+        swap(3, from_far, part, size, 0).start()
+        ring(3, from_far, part, size, 1, down).wait()
+        swap(4, from_far, part, size, 1).start()
+
+    def ring_end(part, size, other_size):
+        for n, h, half in ((0, head, None), (1, from_down, None), (2, from_up, None), (3, from_far, 0), (4, from_far, 1)):
+            swap(n, h, part, size, half).wait_send()
+            swap(n, h + other - core, part, other_size, half).wait_recv()
+
+    ring_first(0, PART_A)
     lax.fori_loop(B_DEV // 2, B_DEV * 3 // 4, prefix, 0)
-
-    from_down, from_up, from_far = down * 2 + core, up * 2 + core, far * 2 + core
-    ring(0, from_down, None, up).wait()
-    ring(2, from_down, 0, up).start()
-    swap(1, from_down, None).start()
-    ring(1, from_up, None, down).wait()
-    ring(3, from_up, 1, down).start()
-    swap(2, from_up, None).start()
-
+    ring_second(0, PART_A)
     lax.fori_loop(B_DEV * 3 // 4, B_DEV, prefix, 0)
+    ring_third(0, PART_A)
+
+    for c in range(2):
+
+        @pl.when(core == c)
+        def _(c=c):
+            def wait_b(i, _):
+                src = lax.rem(me + i, GROUPS)
+                block_b(src, src, src, SIZES[c]).wait()
+                return 0
+
+            lax.fori_loop(1, GROUPS, wait_b, 0)
+            for p in range(PAIRS):
+                parts_b[head, p] = slots_b[par[2 * p] // B_DEV]
+            ring_first(1, SIZES[c])
 
     share(0, left, 0, COLS, right).wait()
     share(2, left, 0, COLS // 2, right).start()
     share(1, right, 0, COLS, left).wait()
     share(3, right, COLS // 2, COLS // 2, left).start()
 
-    ring(2, from_far, 0, up).wait()
-    swap(3, from_far, 0).start()
-    ring(3, from_far, 1, down).wait()
-    swap(4, from_far, 1).start()
-    other = 1 - core
-    swap(0, y * 2 + other, None).wait()
-    swap(1, down * 2 + other, None).wait()
-    swap(2, up * 2 + other, None).wait()
-    swap(3, far * 2 + other, 0).wait()
-    swap(4, far * 2 + other, 1).wait()
-
-    def gather(p, _):
-        for yy in range(NY):
-            fork[p, yy * 144:yy * 144 + 80] = parts[2 * yy, p]
-            fork[p, yy * 144 + 80:yy * 144 + 144] = parts[2 * yy + 1, p, 16:80]
-        return 0
-
-    lax.fori_loop(0, PAIRS, gather, 0)
-
-    def forked(p, _):
-        rows = pl.ds(pl.multiple_of(p * 128, 128), 128)
-        keys = fork[p]
-        s = scores(rows, keys) * SCALE
-        old = peak[rows, :][:, :1]
-        m = jnp.maximum(jnp.max(s, axis=1, keepdims=True), old)
-        w = jnp.exp(s - m).astype(BF)
-        back = jnp.exp(old - m)
-        norm = total[rows, :][:, :1] * back + jnp.sum(w.astype(F32), axis=1, keepdims=True)
-        c = dot_nt(w, keys[:LAT])
-        scale = 1.0 / norm
-        for j in range(LANES):
-            both = (ctx[j, rows, :] * back + c[:, j * 128:(j + 1) * 128]) * scale
-            ctx[j, rows, :] = both.astype(BF).astype(F32)
+    for c in range(2):
+
+        @pl.when(core == c)
+        def _(c=c):
+            ring_second(1, SIZES[c])
+            ring_third(1, SIZES[c])
+            ring_end(1, SIZES[c], SIZES[1 - c])
+
+    ring_end(0, PART_A, PART_A)
+
+    def forked(n, _):
+        several = range(TOGETHER)
+        rows = [pl.ds(pl.multiple_of((n * TOGETHER + i) * 128, 128), 128) for i in several]
+        keys = []
+        for i in several:
+            p = n * TOGETHER + i
+            found = []
+            for yy in range(NY):
+                found += [parts_a[2 * yy, p], parts_b[2 * yy, p], parts_a[2 * yy + 1, p], parts_b[2 * yy + 1, p, :SIZES[1]]]
+            keys.append(jnp.concatenate(found, axis=0))
+        s = [scores(rows[i], keys[i]) * SCALE for i in several]
+        old = [peak[rows[i], :][:, :1] for i in several]
+        m = [jnp.maximum(jnp.max(s[i], axis=1, keepdims=True), old[i]) for i in several]
+        w = [jnp.exp(s[i] - m[i]).astype(BF) for i in several]
+        back = [jnp.exp(old[i] - m[i]) for i in several]
+        norm = [
+            total[rows[i], :][:, :1] * back[i] + jnp.sum(w[i].astype(F32), axis=1, keepdims=True) for i in several
+        ]
+        c = [dot_nt(w[i], keys[i][:LAT]) for i in several]
+        scale = [1.0 / norm[i] for i in several]
+        both = [
+            [(ctx[j, rows[i], :] * back[i] + c[i][:, j * 128:(j + 1) * 128]) * scale[i] for j in range(LANES)]
+            for i in several
+        ]
+        for i in several:
+            for j in range(LANES):
+                ctx[j, rows[i], :] = both[i][j].astype(BF).astype(F32)
         return 0
 
     def half_of(slot, s):
@@ -281,7 +374,7 @@
 
     loads[9].wait()
     for s in (0, 1):
-        lax.fori_loop(s * (PAIRS // 2), (s + 1) * (PAIRS // 2), forked, 0)
+        lax.fori_loop(s * (PAIRS // 2) // TOGETHER, (s + 1) * (PAIRS // 2) // TOGETHER, forked, 0)
         for h in range(HEADS):
             c = [ctx[j, pl.ds(s * HALF * HEADS + h, HALF, stride=HEADS), :] for j in range(LANES)]
             c = jnp.concatenate(c, axis=1).astype(BF)
@@ -292,17 +385,57 @@
     share(2, lax.rem(x + 2, NX), 0, COLS // 2, right).wait()
     share(3, lax.rem(x + 2, NX), COLS // 2, COLS // 2, left).wait()
 
-    def reduce_copy(slot):
-        return remote(made.at[slot], landed.at[head], r_send.at[slot], r_recv.at[head], head=lax.rem(z + 8 - slot, 8))
+    def reduce_copy(slot, to):
+        return remote(made.at[slot, to], landed.at[slot, head], r_send.at[slot, to], r_recv.at[slot, head], head=to)
 
     def multiply(slot):
-        made[slot] = dot_nt(held[slot], wt[...]).astype(BF)
-
-        @pl.when(lax.rem(z + 8 - slot, 8) != head)
+        for g in range(NX):
+            r = dot_nt(held[slot], wt[g * COLS:(g + 1) * COLS]).astype(BF)
+            for n in range(2):
+                to = 2 * g + n
+                made[slot, to] = r[:, n * SLICE:(n + 1) * SLICE]
+
+                @pl.when(to != head)
+                def _(to=to):
+                    reduce_copy(slot, to).start()
+
+    def is_mine(slot):
+        return (y == x) & (lax.rem(z + 8 - slot, 8) == head)
+
+    def final_copy(slot):
+        return remote(
+            done.at[slot], final.at[x, core], f_send.at[slot], f_recv.at[x, core],
+            branch=z * NX + y, head=lax.rem(z + 8 - slot, 8),
+        )
+
+    def fold(slot):
+        acc = made[slot, head].astype(F32)
+        for i in range(1, 8):
+            src = lax.rem(head + i, 8)
+            remote(
+                made.at[slot, src], landed.at[slot, src], r_send.at[slot, src], r_recv.at[slot, src], head=src
+            ).wait_recv()
+            acc = acc + landed[slot, src].astype(F32)
+        done[slot] = acc.astype(BF)
+        mine_too = is_mine(slot)
+
+        @pl.when(mine_too)
         def _():
-            reduce_copy(slot).start()
-
-    multiply(0)
+            final[x, core] = done[slot]
+
+        @pl.when(~mine_too)
+        def _():
+            final_copy(slot).start()
+
+    waiting = []
+
+    def turn(slot):
+        multiply(slot)
+        waiting.append(slot)
+        if len(waiting) > LAG:
+            fold(waiting.pop(0))
+
+    turn(0)
     for k in (1, 2, 3):
         for s in (0, 1):
             for way in (0, 1):
@@ -311,43 +444,39 @@
                 if k < 3 or t == way:
                     go(way, k + 1, t)
             if s == 0 and k > 1:
-                multiply(9 - k)
-        multiply(k)
-    multiply(5)
+                turn(9 - k)
+        turn(k)
+    turn(5)
     hop(0, 4, 0).wait_recv()
     hop(1, 4, 1).wait_recv()
-    multiply(4)
-
-    acc = made[lax.rem(z + 8 - head, 8)].astype(F32)
-    for i in range(1, 8):
-        src = lax.rem(head + i, 8)
-        remote(made.at[0], landed.at[src], r_send.at[0], r_recv.at[src], head=src).wait_recv()
-        acc = acc + landed[src].astype(F32)
-    acc = acc.astype(BF)
+    turn(4)
+    for slot in waiting:
+        fold(slot)
+
     for i in range(NX):
-        cut[i] = acc[:, i * COLS:(i + 1) * COLS]
-    final[x] = cut[x]
-    spread = []
-    for i in range(1, NX):
-        d = lax.rem(x + i, NX)
-        c = remote(cut.at[d], final.at[x], x_send.at[i], x_recv.at[x], branch=z * NX + d)
-        c.start()
-        spread.append(c)
-    for i in range(1, NX):
-        d = lax.rem(x + i, NX)
-        remote(cut.at[d], final.at[d], x_send.at[i], x_recv.at[d], branch=z * NX + d).wait_recv()
-    for i in range(NX):
-        out[i * ROWS:(i + 1) * ROWS, :] = final[i]
+        for n in range(2):
+
+            @pl.when((i != x) | (2 * x + n != head))
+            def _(i=i, n=n):
+                remote(
+                    done.at[0], final.at[i, n], f_send.at[0], f_recv.at[i, n], branch=z * NX + i, head=2 * x + n
+                ).wait_recv()
+
+        out[i * ROWS:(i + 1) * ROWS, :] = jnp.concatenate([final[i, 0], final[i, 1]], axis=1)
 
     for c in hops:
         c.wait_send()
-    for c in spread:
-        c.wait_send()
     for slot in range(8):
 
-        @pl.when(lax.rem(z + 8 - slot, 8) != head)
+        @pl.when(~is_mine(slot))
         def _(slot=slot):
-            reduce_copy(slot).wait_send()
+            final_copy(slot).wait_send()
+
+        def sent(i, _, slot=slot):
+            reduce_copy(slot, lax.rem(head + i, 8)).wait_send()
+            return 0
+
+        lax.fori_loop(1, 8, sent, 0)
 
 
 def layer(*operands):
@@ -374,22 +503,23 @@
             vmem((QROWS, 128), F32),
             vmem((B_DEV, PART, 128), BF),
             vmem((GROUPS, PART, 128), BF),
-            vmem((GROUPS, PART, 128), BF),
+            vmem((GROUPS, PART_A, 128), BF),
+            vmem((GROUPS, PART_B, 128), BF),
             vmem((1, 128), jnp.int32),
             vmem((GROUPS, 1, 128), jnp.int32),
             vmem((GROUPS, 1, 128), jnp.int32),
             smem((GROUPS, 1, 128), jnp.int32),
-            vmem((8, PAIRS, PART, 128), BF),
-            vmem((PAIRS, WIDTH, BLOCK), BF),
+            vmem((8, PAIRS, PART_A, 128), BF),
+            vmem((8, PAIRS, PART_B, 128), BF),
             vmem((8, ROWS, HEADS * VDIM), BF),
-            vmem((8, ROWS, NX * COLS), BF),
-            vmem((8, ROWS, NX * COLS), BF),
-            vmem((NX, ROWS, COLS), BF),
-            vmem((NX, ROWS, COLS), BF),
-            dma((11,)), dma,
-            dma((GROUPS,)), dma((GROUPS,)), dma((GROUPS,)), dma((GROUPS,)),
-            dma((4,)), dma((4,)), dma((5,)), dma((5,)),
-            dma((4,)), dma((4,)), dma((2, 4, 2)), dma((2, 4, 2)), dma((8,)), dma((8,)), dma((NX,)), dma((NX,)),
+            vmem((8, 8, ROWS, SLICE), BF),
+            vmem((8, 8, ROWS, SLICE), BF),
+            vmem((8, ROWS, SLICE), BF),
+            vmem((NX, 2, ROWS, SLICE), BF),
+            dma((12,)), dma,
+            dma((GROUPS,)), dma((GROUPS,)), dma((2, GROUPS)), dma((2, GROUPS)),
+            dma((2, 4)), dma((2, 4)), dma((2, 5)), dma((2, 5)),
+            dma((4,)), dma((4,)), dma((2, 4, 2)), dma((2, 4, 2)), dma((8, 8)), dma((8, 8)), dma((8,)), dma((NX, 2)),
         ],
         compiler_params=pltpu.CompilerParams(
             collective_id=0, has_side_effects=True, vmem_limit_bytes=VMEM_BYTES

time: 106 us -> 109 us (1.028)
  Pallas kernels: 103 us -> 106 us
    pallas_call x1, Pallas kernels: 103 us -> 106 us  [layer(): pl.pallas_call(layer_kernel, out_shape=jax.ShapeDtypeStruct((NX * ROWS, C...]
where the time goes in v3:
time: 109 us; the launch traced here: 108 us
  Pallas kernels  106 us (97%)
  local copies, waits for them, and re-layouts  1.73 us (2%)
    pallas_call x1, Pallas kernels, layer(): pl.pallas_call(layer_kernel, out_shape=jax.ShapeDtypeStruct((NX * ROWS, C...  106 us

profile of v3, /device:TPU:18, one launch (start us, length us, event | category | flops | bytes accessed | tf_op | source)
XLA Modules:
  0.0 107.6 jit_solution(8572454323143922948)
XLA Ops:
  0.0 105.9 %shard_map.109 = bf16[384,224]{1,0:T(8,128)(2,1)} custom-call(s32[24]{0:T(128)} %par_hbm.1, s32[24]{0:T(128)} %lens_hbm.1, s32[24]{0:T(128)} %bitcast.7, bf16[96,2048]{1,0:T(8,128)(2,1)} %qn_hbm.1, bf16[96,1024]{1,0:T(8,128)(2,1)} %qr_hbm.1, bf16[16,128,512]{2,1,0:T(8,128)(2,1)} %ku_hbm.1, bf16[16,512,128]{2,1,0:T(8,128)(2,1)} %vu_hbm.1, ...), custom_call_target="tpu_custom_call" | custom-call | flops 4200000000 | bytes 16000000 | tf_op jit(solution)/shard_map/pallas_call | solution.py:485
  105.9 1.7 %copy.12 = bf16[384,224]{0,1:T(8,128)(2,1)} copy(bf16[384,224]{1,0:T(8,128)(2,1)} %shard_map.109) | data formatting | bytes 344064 | tf_op jit(solution)/shard_map/pallas_call | solution.py:485

commit v4 on v3

--- a/solution.py
+++ b/solution.py
@@ -23,13 +23,12 @@
 COLS = 224
 NZ, NX, NY = 8, 4, 4
 GROUPS = NZ * NX
-PART_A, PART_B = 48, 32
-PART = PART_A + PART_B
+PART = 80
+CHUNK = PAIRS // 2
 SLICE = COLS // 2
 VMEM_BYTES = 60 * 2**20
 LANES = LAT // 128
-TOGETHER = 3
-LAG = 2
+TOGETHER = 1
 SCALE = (NOPE + ROPE) ** -0.5
 BF = jnp.bfloat16
 F32 = jnp.float32
@@ -37,7 +36,8 @@
 NT = (((1,), (1,)), ((), ()))
 
 
-SIZES = (32, 16)
+SIZES = (80, 64)
+ORDER = (0, 3, 1, 2)
 
 
 def dot(a, b):
@@ -62,8 +62,8 @@
     par, lens, table,
     qn, qr, ku, vu, pool, nl, nlt, wt,
     qs, ctx, peak, total,
-    mine, packed, slots_a, slots_b, my_par, all_par, pick_v, pick_s, parts_a, parts_b,
-    held, made, landed, done, final,
+    mine, packed, slots, my_par, all_par, pick_v, pick_s, parts, fork,
+    held, made, met, summed, done, final,
     load_sem, pick_sem, par_send, par_recv, out_send, out_recv, ring_send, ring_recv, core_send, core_recv,
     w_send, w_recv, z_send, z_recv, r_send, r_recv, f_send, f_recv,
 ):
@@ -169,37 +169,24 @@
 
     pick.wait()
 
-    def block_a(n, at, to):
-        return remote(packed.at[n, pl.ds(0, PART_A)], slots_a.at[at], out_send.at[0, n], out_recv.at[0, at], branch=to)
-
-    def block_b(n, at, to, size):
+    def block(n, at, to, size):
         return remote(
-            packed.at[n, pl.ds(PART_A, size)], slots_b.at[at, pl.ds(0, size)],
-            out_send.at[1, n], out_recv.at[1, at], branch=to,
+            packed.at[n, pl.ds(0, size)], slots.at[at, pl.ds(0, size)], out_send.at[n], out_recv.at[at], branch=to
         )
-
-    def send_a(i, _):
-        d = lax.rem(me + i, GROUPS)
-        packed[d] = mine[pick_s[d, 0, 0]]
-        block_a(d, me, d).start()
-        return 0
-
-    lax.fori_loop(1, GROUPS, send_a, 0)
 
     for c in range(2):
 
         @pl.when(core == c)
         def _(c=c):
-            def send_b(i, _):
+            def send_block(i, _):
                 d = lax.rem(me + i, GROUPS)
-                block_b(d, me, d, SIZES[c]).start()
+                packed[d] = mine[pick_s[d, 0, 0]]
+                block(d, me, d, SIZES[c]).start()
                 return 0
 
-            lax.fori_loop(1, GROUPS, send_b, 0)
-
-    own = mine[pick_s[me, 0, 0]]
-    slots_a[me] = own[:PART_A]
-    slots_b[me] = own[PART_A:]
+            lax.fori_loop(1, GROUPS, send_block, 0)
+
+    slots[me] = mine[pick_s[me, 0, 0]]
 
     loads[10].wait()
 
@@ -243,99 +230,95 @@
 
     lax.fori_loop(0, B_DEV // 2, prefix, 0)
 
-    def wait_a(i, _):
-        src = lax.rem(me + i, GROUPS)
-        block_a(src, src, src).wait()
-        return 0
-
-    lax.fori_loop(1, GROUPS, wait_a, 0)
-    for p in range(PAIRS):
-        parts_a[head, p] = slots_a[par[2 * p] // B_DEV]
-
     from_down, from_up, from_far = down * 2 + core, up * 2 + core, far * 2 + core
     other = 1 - core
 
-    def piece(h, part, size, half):
-        at = parts_a.at[h] if part == 0 else parts_b.at[h, :, pl.ds(0, size)]
-        return at if half is None else at.at[pl.ds(half * (PAIRS // 2), PAIRS // 2)]
-
-    def ring(n, h, part, size, half, to):
-        at = piece(h, part, size, half)
-        return remote(at, at, ring_send.at[part, n], ring_recv.at[part, n], head=to * 2 + core)
-
-    def swap(n, h, part, size, half):
-        at = piece(h, part, size, half)
-        return remote(at, at, core_send.at[part, n], core_recv.at[part, n], head=y * 2 + other)
-
-    def ring_first(part, size):
-        ring(0, head, part, size, None, up).start()
-        ring(1, head, part, size, None, down).start()
-        swap(0, head, part, size, None).start()
-
-    def ring_second(part, size):
-        ring(0, from_down, part, size, None, up).wait()
-        ring(2, from_down, part, size, 0, up).start()
-        ring(1, from_up, part, size, None, down).wait()
-        ring(3, from_up, part, size, 1, down).start()
-        swap(1, from_down, part, size, None).start()
-        swap(2, from_up, part, size, None).start()
-
-    def ring_third(part, size):
-        ring(2, from_far, part, size, 0, up).wait()
-        swap(3, from_far, part, size, 0).start()
-        ring(3, from_far, part, size, 1, down).wait()
-        swap(4, from_far, part, size, 1).start()
-
-    def ring_end(part, size, other_size):
+    def piece(h, ch, size, half):
+        first, count = (ch * CHUNK, CHUNK) if half is None else (ch * CHUNK + half * (CHUNK // 2), CHUNK // 2)
+        return parts.at[h, pl.ds(first, count), pl.ds(0, size)]
+
+    def ring(n, h, ch, size, half, to):
+        at = piece(h, ch, size, half)
+        return remote(at, at, ring_send.at[ch, n], ring_recv.at[ch, n], head=to * 2 + core)
+
+    def swap(n, h, ch, size, half):
+        at = piece(h, ch, size, half)
+        return remote(at, at, core_send.at[ch, n], core_recv.at[ch, n], head=y * 2 + other)
+
+    def ring_first(ch, size):
+        ring(0, head, ch, size, None, up).start()
+        ring(1, head, ch, size, None, down).start()
+        swap(0, head, ch, size, None).start()
+
+    def ring_second(ch, size):
+        ring(0, from_down, ch, size, None, up).wait()
+        ring(2, from_down, ch, size, 0, up).start()
+        ring(1, from_up, ch, size, None, down).wait()
+        ring(3, from_up, ch, size, 1, down).start()
+        swap(1, from_down, ch, size, None).start()
+        swap(2, from_up, ch, size, None).start()
+
+    def ring_third(ch, size):
+        ring(2, from_far, ch, size, 0, up).wait()
+        swap(3, from_far, ch, size, 0).start()
+        ring(3, from_far, ch, size, 1, down).wait()
+        swap(4, from_far, ch, size, 1).start()
+
+    def ring_end(ch, size, other_size):
         for n, h, half in ((0, head, None), (1, from_down, None), (2, from_up, None), (3, from_far, 0), (4, from_far, 1)):
-            swap(n, h, part, size, half).wait_send()
-            swap(n, h + other - core, part, other_size, half).wait_recv()
-
-    ring_first(0, PART_A)
-    lax.fori_loop(B_DEV // 2, B_DEV * 3 // 4, prefix, 0)
-    ring_second(0, PART_A)
-    lax.fori_loop(B_DEV * 3 // 4, B_DEV, prefix, 0)
-    ring_third(0, PART_A)
+            swap(n, h, ch, size, half).wait_send()
+            swap(n, h + other - core, ch, other_size, half).wait_recv()
 
     for c in range(2):
 
         @pl.when(core == c)
         def _(c=c):
-            def wait_b(i, _):
+            def wait_block(i, _):
                 src = lax.rem(me + i, GROUPS)
-                block_b(src, src, src, SIZES[c]).wait()
+                block(src, src, src, SIZES[c]).wait()
                 return 0
 
-            lax.fori_loop(1, GROUPS, wait_b, 0)
-            for p in range(PAIRS):
-                parts_b[head, p] = slots_b[par[2 * p] // B_DEV]
-            ring_first(1, SIZES[c])
+            lax.fori_loop(1, GROUPS, wait_block, 0)
+            for ch in range(2):
+                for p in range(ch * CHUNK, (ch + 1) * CHUNK):
+                    parts[head, p] = slots[par[2 * p] // B_DEV]
+                ring_first(ch, SIZES[c])
+
+    lax.fori_loop(B_DEV // 2, B_DEV, prefix, 0)
+
+    for c in range(2):
+
+        @pl.when(core == c)
+        def _(c=c):
+            ring_second(0, SIZES[c])
+            ring_second(1, SIZES[c])
+            ring_third(0, SIZES[c])
+            ring_third(1, SIZES[c])
 
     share(0, left, 0, COLS, right).wait()
     share(2, left, 0, COLS // 2, right).start()
     share(1, right, 0, COLS, left).wait()
     share(3, right, COLS // 2, COLS // 2, left).start()
 
-    for c in range(2):
-
-        @pl.when(core == c)
-        def _(c=c):
-            ring_second(1, SIZES[c])
-            ring_third(1, SIZES[c])
-            ring_end(1, SIZES[c], SIZES[1 - c])
-
-    ring_end(0, PART_A, PART_A)
+    def arrive(ch):
+        for c in range(2):
+
+            @pl.when(core == c)
+            def _(c=c):
+                ring_end(ch, SIZES[c], SIZES[1 - c])
+
+        def gather(p, _):
+            for yy in range(NY):
+                fork[p, yy * 144:yy * 144 + 80] = parts[2 * yy, p]
+                fork[p, yy * 144 + 80:yy * 144 + 144] = parts[2 * yy + 1, p, :64]
+            return 0
+
+        lax.fori_loop(ch * CHUNK, (ch + 1) * CHUNK, gather, 0)
 
     def forked(n, _):
         several = range(TOGETHER)
         rows = [pl.ds(pl.multiple_of((n * TOGETHER + i) * 128, 128), 128) for i in several]
-        keys = []
-        for i in several:
-            p = n * TOGETHER + i
-            found = []
-            for yy in range(NY):
-                found += [parts_a[2 * yy, p], parts_b[2 * yy, p], parts_a[2 * yy + 1, p], parts_b[2 * yy + 1, p, :SIZES[1]]]
-            keys.append(jnp.concatenate(found, axis=0))
+        keys = [fork[n * TOGETHER + i] for i in several]
         s = [scores(rows[i], keys[i]) * SCALE for i in several]
         old = [peak[rows[i], :][:, :1] for i in several]
         m = [jnp.maximum(jnp.max(s[i], axis=1, keepdims=True), old[i]) for i in several]
@@ -374,6 +357,7 @@
 
     loads[9].wait()
     for s in (0, 1):
+        arrive(s)
         lax.fori_loop(s * (PAIRS // 2) // TOGETHER, (s + 1) * (PAIRS // 2) // TOGETHER, forked, 0)
         for h in range(HEADS):
             c = [ctx[j, pl.ds(s * HALF * HEADS + h, HALF, stride=HEADS), :] for j in range(LANES)]
@@ -385,19 +369,42 @@
     share(2, lax.rem(x + 2, NX), 0, COLS // 2, right).wait()
     share(3, lax.rem(x + 2, NX), COLS // 2, COLS // 2, left).wait()
 
-    def reduce_copy(slot, to):
-        return remote(made.at[slot, to], landed.at[slot, head], r_send.at[slot, to], r_recv.at[slot, head], head=to)
+    group = jnp.where((y == 0) | (y == 3), 0, 1)
+    near = jnp.where(lax.rem(y, 2) == 0, y + 1, y - 1)
+    upper = y // 2
+
+    def halve(n, slot):
+        if n == 0:
+            return remote(
+                made.at[slot, other], met.at[slot, pl.ds(0, 4)], r_send.at[0, slot], r_recv.at[0, slot], head=y * 2 + other
+            )
+        if n == 1:
+            return remote(
+                summed.at[slot, pl.ds(2 * (1 - group), 2)], met.at[slot, pl.ds(4, 2)],
+                r_send.at[1, slot], r_recv.at[1, slot], head=near * 2 + core,
+            )
+        return remote(
+            summed.at[slot, 4 + 1 - upper], met.at[slot, 6], r_send.at[2, slot], r_recv.at[2, slot], head=(3 - y) * 2 + core
+        )
 
     def multiply(slot):
-        for g in range(NX):
+        for i, g in enumerate(ORDER):
             r = dot_nt(held[slot], wt[g * COLS:(g + 1) * COLS]).astype(BF)
             for n in range(2):
-                to = 2 * g + n
-                made[slot, to] = r[:, n * SLICE:(n + 1) * SLICE]
-
-                @pl.when(to != head)
-                def _(to=to):
-                    reduce_copy(slot, to).start()
+                made[slot, n, i] = r[:, n * SLICE:(n + 1) * SLICE]
+        halve(0, slot).start()
+
+    def fold_core(slot):
+        halve(0, slot).wait_recv()
+        for i in range(4):
+            summed[slot, i] = (made[slot, core, i].astype(F32) + met[slot, i].astype(F32)).astype(BF)
+        halve(1, slot).start()
+
+    def fold_near(slot):
+        halve(1, slot).wait_recv()
+        for i in range(2):
+            summed[slot, 4 + i] = (summed[slot, 2 * group + i].astype(F32) + met[slot, 4 + i].astype(F32)).astype(BF)
+        halve(2, slot).start()
 
     def is_mine(slot):
         return (y == x) & (lax.rem(z + 8 - slot, 8) == head)
@@ -409,14 +416,8 @@
         )
 
     def fold(slot):
-        acc = made[slot, head].astype(F32)
-        for i in range(1, 8):
-            src = lax.rem(head + i, 8)
-            remote(
-                made.at[slot, src], landed.at[slot, src], r_send.at[slot, src], r_recv.at[slot, src], head=src
-            ).wait_recv()
-            acc = acc + landed[slot, src].astype(F32)
-        done[slot] = acc.astype(BF)
+        halve(2, slot).wait_recv()
+        done[slot] = (summed[slot, 4 + upper].astype(F32) + met[slot, 6].astype(F32)).astype(BF)
         mine_too = is_mine(slot)
 
         @pl.when(mine_too)
@@ -427,13 +428,14 @@
         def _():
             final_copy(slot).start()
 
-    waiting = []
+    order = (0, 1, 7, 2, 6, 3, 5, 4)
 
     def turn(slot):
+        n = order.index(slot)
         multiply(slot)
-        waiting.append(slot)
-        if len(waiting) > LAG:
-            fold(waiting.pop(0))
+        for lag, step in ((1, fold_core), (2, fold_near), (3, fold)):
+            if n >= lag:
+                step(order[n - lag])
 
     turn(0)
     for k in (1, 2, 3):
@@ -450,8 +452,12 @@
     hop(0, 4, 0).wait_recv()
     hop(1, 4, 1).wait_recv()
     turn(4)
-    for slot in waiting:
-        fold(slot)
+    fold_core(4)
+    fold_near(5)
+    fold(3)
+    fold_near(4)
+    fold(5)
+    fold(4)
 
     for i in range(NX):
         for n in range(2):
@@ -472,11 +478,8 @@
         def _(slot=slot):
             final_copy(slot).wait_send()
 
-        def sent(i, _, slot=slot):
-            reduce_copy(slot, lax.rem(head + i, 8)).wait_send()
-            return 0
-
-        lax.fori_loop(1, 8, sent, 0)
+        for n in range(3):
+            halve(n, slot).wait_send()
 
 
 def layer(*operands):
@@ -503,23 +506,23 @@
             vmem((QROWS, 128), F32),
             vmem((B_DEV, PART, 128), BF),
             vmem((GROUPS, PART, 128), BF),
-            vmem((GROUPS, PART_A, 128), BF),
-            vmem((GROUPS, PART_B, 128), BF),
+            vmem((GROUPS, PART, 128), BF),
             vmem((1, 128), jnp.int32),
             vmem((GROUPS, 1, 128), jnp.int32),
             vmem((GROUPS, 1, 128), jnp.int32),
             smem((GROUPS, 1, 128), jnp.int32),
-            vmem((8, PAIRS, PART_A, 128), BF),
-            vmem((8, PAIRS, PART_B, 128), BF),
+            vmem((8, PAIRS, PART, 128), BF),
+            vmem((PAIRS, WIDTH, BLOCK), BF),
             vmem((8, ROWS, HEADS * VDIM), BF),
-            vmem((8, 8, ROWS, SLICE), BF),
-            vmem((8, 8, ROWS, SLICE), BF),
+            vmem((8, 2, NY, ROWS, SLICE), BF),
+            vmem((8, 7, ROWS, SLICE), BF),
+            vmem((8, 6, ROWS, SLICE), BF),
             vmem((8, ROWS, SLICE), BF),
             vmem((NX, 2, ROWS, SLICE), BF),
             dma((12,)), dma,
-            dma((GROUPS,)), dma((GROUPS,)), dma((2, GROUPS)), dma((2, GROUPS)),
+            dma((GROUPS,)), dma((GROUPS,)), dma((GROUPS,)), dma((GROUPS,)),
             dma((2, 4)), dma((2, 4)), dma((2, 5)), dma((2, 5)),
-            dma((4,)), dma((4,)), dma((2, 4, 2)), dma((2, 4, 2)), dma((8, 8)), dma((8, 8)), dma((8,)), dma((NX, 2)),
+            dma((4,)), dma((4,)), dma((2, 4, 2)), dma((2, 4, 2)), dma((3, 8)), dma((3, 8)), dma((8,)), dma((NX, 2)),
         ],
         compiler_params=pltpu.CompilerParams(
             collective_id=0, has_side_effects=True, vmem_limit_bytes=VMEM_BYTES

time: 109 us -> 105 us (0.963); the launches traced: 108 us -> 105 us
  Pallas kernels: 106 us -> 103 us
    pallas_call x1, Pallas kernels: 106 us -> 103 us  [layer(): pl.pallas_call(layer_kernel, out_shape=jax.ShapeDtypeStruct((NX * ROWS, C...]
where the time goes in v4:
time: 105 us
  Pallas kernels  103 us (98%)
  local copies, waits for them, and re-layouts  1.73 us (2%)
    pallas_call x1, Pallas kernels, layer(): pl.pallas_call(layer_kernel, out_shape=jax.ShapeDtypeStruct((NX * ROWS, C...  103 us

profile of v4, /device:TPU:18, one launch (start us, length us, event | category | flops | bytes accessed | tf_op | source)
XLA Modules:
  0.0 105.1 jit_solution(10067265157465681485)
XLA Ops:
  0.0 103.4 %shard_map.109 = bf16[384,224]{1,0:T(8,128)(2,1)} custom-call(s32[24]{0:T(128)} %par_hbm.1, s32[24]{0:T(128)} %lens_hbm.1, s32[24]{0:T(128)} %bitcast.7, bf16[96,2048]{1,0:T(8,128)(2,1)} %qn_hbm.1, bf16[96,1024]{1,0:T(8,128)(2,1)} %qr_hbm.1, bf16[16,128,512]{2,1,0:T(8,128)(2,1)} %ku_hbm.1, bf16[16,512,128]{2,1,0:T(8,128)(2,1)} %vu_hbm.1, ...), custom_call_target="tpu_custom_call" | custom-call | flops 4200000000 | bytes 16000000 | tf_op jit(solution)/shard_map/pallas_call | solution.py:488
  103.4 1.7 %copy.12 = bf16[384,224]{0,1:T(8,128)(2,1)} copy(bf16[384,224]{1,0:T(8,128)(2,1)} %shard_map.109) | data formatting | bytes 344064 | tf_op jit(solution)/shard_map/pallas_call | solution.py:488

commit v5 on v4

--- a/solution.py
+++ b/solution.py
@@ -26,6 +26,7 @@
 PART = 80
 CHUNK = PAIRS // 2
 SLICE = COLS // 2
+PADDED = 128
 VMEM_BYTES = 60 * 2**20
 LANES = LAT // 128
 TOGETHER = 1
@@ -78,12 +79,13 @@
     prv = lax.rem(z + NZ - 1, NZ) * NX + x
     row0 = pl.multiple_of(y * 144 + core * PART, 16)
 
-    def columns(i, start=0, size=COLS):
-        return wt.at[pl.ds(pl.multiple_of(i * COLS + start, 16), size)]
+    def columns(i, n):
+        return wt.at[pl.ds(pl.multiple_of((2 * i + n) * PADDED, PADDED), SLICE)]
 
     pairs = (
         (par_hbm, par), (recent_hbm.at[:, pl.ds(row0, 64), :], mine.at[:, pl.ds(0, 64), :]), (ku_hbm, ku), (qn_hbm, qn), (qr_hbm, qr),
-        (lens_hbm, lens), (table_hbm, table), (pool_hbm, pool), (nl_hbm, nl), (vu_hbm, vu), (w_hbm, columns(x)),
+        (lens_hbm, lens), (table_hbm, table), (pool_hbm, pool), (nl_hbm, nl), (vu_hbm, vu), (w_hbm.at[pl.ds(0, SLICE)], columns(x, 0)),
+        (w_hbm.at[pl.ds(SLICE, SLICE)], columns(x, 1)),
     )
     loads = [pltpu.make_async_copy(src, dst, load_sem.at[i]) for i, (src, dst) in enumerate(pairs)]
     for load in loads:
@@ -91,7 +93,7 @@
 
     def extra():
         return pltpu.make_async_copy(
-            recent_hbm.at[:, pl.ds(pl.multiple_of(y * 144 + 64, 16), 16), :], mine.at[:, pl.ds(64, 16), :], load_sem.at[11]
+            recent_hbm.at[:, pl.ds(pl.multiple_of(y * 144 + 64, 16), 16), :], mine.at[:, pl.ds(64, 16), :], load_sem.at[12]
         )
 
     @pl.when(core == 0)
@@ -188,15 +190,17 @@
 
     slots[me] = mine[pick_s[me, 0, 0]]
 
+    for i in range(2 * NX):
+        wt[i * PADDED + SLICE:(i + 1) * PADDED, :] = jnp.zeros((PADDED - SLICE, HEADS * VDIM), BF)
     loads[10].wait()
-
-    def share(n, owner, start, size, to):
-        return remote(
-            columns(owner, start, size), columns(owner, start, size), w_send.at[n], w_recv.at[n], branch=z * NX + to
-        )
-
-    share(0, x, 0, COLS, right).start()
-    share(1, x, 0, COLS, left).start()
+    loads[11].wait()
+
+    def share(m, owner, n, to):
+        return remote(columns(owner, n), columns(owner, n), w_send.at[m], w_recv.at[m], branch=z * NX + to)
+
+    for n in range(2):
+        share(n, x, n, right).start()
+        share(2 + n, x, n, left).start()
 
     for n in (5, 6, 7, 8):
         loads[n].wait()
@@ -295,10 +299,12 @@
             ring_third(0, SIZES[c])
             ring_third(1, SIZES[c])
 
-    share(0, left, 0, COLS, right).wait()
-    share(2, left, 0, COLS // 2, right).start()
-    share(1, right, 0, COLS, left).wait()
-    share(3, right, COLS // 2, COLS // 2, left).start()
+    share(0, left, 0, right).wait()
+    share(4, left, 0, right).start()
+    share(3, right, 1, left).wait()
+    share(5, right, 1, left).start()
+    share(1, left, 1, right).wait()
+    share(2, right, 0, left).wait()
 
     def arrive(ch):
         for c in range(2):
@@ -366,8 +372,8 @@
         go(0, 1, s)
         go(1, 1, s)
 
-    share(2, lax.rem(x + 2, NX), 0, COLS // 2, right).wait()
-    share(3, lax.rem(x + 2, NX), COLS // 2, COLS // 2, left).wait()
+    share(4, lax.rem(x + 2, NX), 0, right).wait()
+    share(5, lax.rem(x + 2, NX), 1, left).wait()
 
     group = jnp.where((y == 0) | (y == 3), 0, 1)
     near = jnp.where(lax.rem(y, 2) == 0, y + 1, y - 1)
@@ -389,9 +395,9 @@
 
     def multiply(slot):
         for i, g in enumerate(ORDER):
-            r = dot_nt(held[slot], wt[g * COLS:(g + 1) * COLS]).astype(BF)
+            r = dot_nt(held[slot], wt[g * 2 * PADDED:(g + 1) * 2 * PADDED]).astype(BF)
             for n in range(2):
-                made[slot, n, i] = r[:, n * SLICE:(n + 1) * SLICE]
+                made[slot, n, i] = r[:, n * PADDED:(n + 1) * PADDED]
         halve(0, slot).start()
 
     def fold_core(slot):
@@ -468,7 +474,7 @@
                     done.at[0], final.at[i, n], f_send.at[0], f_recv.at[i, n], branch=z * NX + i, head=2 * x + n
                 ).wait_recv()
 
-        out[i * ROWS:(i + 1) * ROWS, :] = jnp.concatenate([final[i, 0], final[i, 1]], axis=1)
+        out[i * ROWS:(i + 1) * ROWS, :] = jnp.concatenate([final[i, 0][:, :SLICE], final[i, 1][:, :SLICE]], axis=1)
 
     for c in hops:
         c.wait_send()
@@ -499,7 +505,7 @@
             vmem((B_DEV, WIDTH, BLOCK), BF),
             vmem((ROWS, WIDTH), BF),
             vmem((WIDTH, 128), BF),
-            vmem((NX * COLS, HEADS * VDIM), BF),
+            vmem((2 * NX * PADDED, HEADS * VDIM), BF),
             vmem((LANES + 1, QROWS, 128), F32),
             vmem((LANES, QROWS, 128), F32),
             vmem((QROWS, 128), F32),
@@ -514,15 +520,15 @@
             vmem((8, PAIRS, PART, 128), BF),
             vmem((PAIRS, WIDTH, BLOCK), BF),
             vmem((8, ROWS, HEADS * VDIM), BF),
-            vmem((8, 2, NY, ROWS, SLICE), BF),
-            vmem((8, 7, ROWS, SLICE), BF),
-            vmem((8, 6, ROWS, SLICE), BF),
-            vmem((8, ROWS, SLICE), BF),
-            vmem((NX, 2, ROWS, SLICE), BF),
-            dma((12,)), dma,
+            vmem((8, 2, NY, ROWS, PADDED), BF),
+            vmem((8, 7, ROWS, PADDED), BF),
+            vmem((8, 6, ROWS, PADDED), BF),
+            vmem((8, ROWS, PADDED), BF),
+            vmem((NX, 2, ROWS, PADDED), BF),
+            dma((13,)), dma,
             dma((GROUPS,)), dma((GROUPS,)), dma((GROUPS,)), dma((GROUPS,)),
             dma((2, 4)), dma((2, 4)), dma((2, 5)), dma((2, 5)),
-            dma((4,)), dma((4,)), dma((2, 4, 2)), dma((2, 4, 2)), dma((3, 8)), dma((3, 8)), dma((8,)), dma((NX, 2)),
+            dma((6,)), dma((6,)), dma((2, 4, 2)), dma((2, 4, 2)), dma((3, 8)), dma((3, 8)), dma((8,)), dma((NX, 2)),
         ],
         compiler_params=pltpu.CompilerParams(
             collective_id=0, has_side_effects=True, vmem_limit_bytes=VMEM_BYTES

time: 105 us -> 105 us (level)
  no operation moved by 1% of the time
where the time goes in v5:
time: 105 us
  Pallas kernels  103 us (98%)
  local copies, waits for them, and re-layouts  1.73 us (2%)
    pallas_call x1, Pallas kernels, layer(): pl.pallas_call(layer_kernel, out_shape=jax.ShapeDtypeStruct((NX * ROWS, C...  103 us

profile of v5, /device:TPU:18, one launch (start us, length us, event | category | flops | bytes accessed | tf_op | source)
XLA Modules:
  0.0 105.0 jit_solution(7241790117675144089)
XLA Ops:
  0.0 103.2 %shard_map.109 = bf16[384,224]{1,0:T(8,128)(2,1)} custom-call(s32[24]{0:T(128)} %par_hbm.1, s32[24]{0:T(128)} %lens_hbm.1, s32[24]{0:T(128)} %bitcast.7, bf16[96,2048]{1,0:T(8,128)(2,1)} %qn_hbm.1, bf16[96,1024]{1,0:T(8,128)(2,1)} %qr_hbm.1, bf16[16,128,512]{2,1,0:T(8,128)(2,1)} %ku_hbm.1, bf16[16,512,128]{2,1,0:T(8,128)(2,1)} %vu_hbm.1, ...), custom_call_target="tpu_custom_call" | custom-call | flops 4200000000 | bytes 16000000 | tf_op jit(solution)/shard_map/pallas_call | solution.py:494
  103.3 1.7 %copy.12 = bf16[384,224]{0,1:T(8,128)(2,1)} copy(bf16[384,224]{1,0:T(8,128)(2,1)} %shard_map.109) | data formatting | bytes 344064 | tf_op jit(solution)/shard_map/pallas_call | solution.py:494

commit v6 on v5

--- a/solution.py
+++ b/solution.py
@@ -38,7 +38,6 @@
 
 
 SIZES = (80, 64)
-ORDER = (0, 3, 1, 2)
 
 
 def dot(a, b):
@@ -64,7 +63,7 @@
     qn, qr, ku, vu, pool, nl, nlt, wt,
     qs, ctx, peak, total,
     mine, packed, slots, my_par, all_par, pick_v, pick_s, parts, fork,
-    held, made, met, summed, done, final,
+    held, made, met, summed, landed,
     load_sem, pick_sem, par_send, par_recv, out_send, out_recv, ring_send, ring_recv, core_send, core_recv,
     w_send, w_recv, z_send, z_recv, r_send, r_recv, f_send, f_recv,
 ):
@@ -113,14 +112,13 @@
     lax.fori_loop(1, GROUPS, greet, 0)
     for i in range(1, 8):
         pl.semaphore_signal(barrier, inc=1, device_id={"head": lax.rem(head + i, 8)}, device_id_type=MESH)
-    for i in range(NX):
-        for n in range(2):
-
-            @pl.when((i != x) | (2 * x + n != head))
-            def _(i=i, n=n):
-                pl.semaphore_signal(
-                    barrier, inc=1, device_id={"branch": z * NX + i, "head": 2 * x + n}, device_id_type=MESH
-                )
+    for i in range(1, NX):
+        for n in range(1, 8):
+            pl.semaphore_signal(
+                barrier, inc=1,
+                device_id={"branch": z * NX + lax.rem(x + i, NX), "head": lax.rem(head + n, 8)},
+                device_id_type=MESH,
+            )
 
     loads[0].wait()
     lane = lax.broadcasted_iota(jnp.int32, (1, 128), 1)
@@ -129,7 +127,7 @@
         row = jnp.where(lane == b, par[b], row)
     my_par[...] = row
     all_par[me] = row
-    pl.semaphore_wait(barrier, GROUPS - 1 + 7 + jnp.where(y == x, 7, 8))
+    pl.semaphore_wait(barrier, GROUPS - 1 + 7 + 21)
 
     def start_par(i, _):
         d = lax.rem(me + i, GROUPS)
@@ -375,73 +373,47 @@
     share(4, lax.rem(x + 2, NX), 0, right).wait()
     share(5, lax.rem(x + 2, NX), 1, left).wait()
 
-    group = jnp.where((y == 0) | (y == 3), 0, 1)
-    near = jnp.where(lax.rem(y, 2) == 0, y + 1, y - 1)
-    upper = y // 2
-
-    def halve(n, slot):
-        if n == 0:
-            return remote(
-                made.at[slot, other], met.at[slot, pl.ds(0, 4)], r_send.at[0, slot], r_recv.at[0, slot], head=y * 2 + other
-            )
-        if n == 1:
-            return remote(
-                summed.at[slot, pl.ds(2 * (1 - group), 2)], met.at[slot, pl.ds(4, 2)],
-                r_send.at[1, slot], r_recv.at[1, slot], head=near * 2 + core,
-            )
-        return remote(
-            summed.at[slot, 4 + 1 - upper], met.at[slot, 6], r_send.at[2, slot], r_recv.at[2, slot], head=(3 - y) * 2 + core
-        )
+    def swap_sums(slot):
+        return remote(made.at[slot, other], met.at[slot], r_send.at[slot], r_recv.at[slot], head=y * 2 + other)
 
     def multiply(slot):
-        for i, g in enumerate(ORDER):
-            r = dot_nt(held[slot], wt[g * 2 * PADDED:(g + 1) * 2 * PADDED]).astype(BF)
+        for i in range(NX):
+            r = dot_nt(held[slot], wt[i * 2 * PADDED:(i + 1) * 2 * PADDED]).astype(BF)
             for n in range(2):
                 made[slot, n, i] = r[:, n * PADDED:(n + 1) * PADDED]
-        halve(0, slot).start()
-
-    def fold_core(slot):
-        halve(0, slot).wait_recv()
-        for i in range(4):
-            summed[slot, i] = (made[slot, core, i].astype(F32) + met[slot, i].astype(F32)).astype(BF)
-        halve(1, slot).start()
-
-    def fold_near(slot):
-        halve(1, slot).wait_recv()
-        for i in range(2):
-            summed[slot, 4 + i] = (summed[slot, 2 * group + i].astype(F32) + met[slot, 4 + i].astype(F32)).astype(BF)
-        halve(2, slot).start()
-
-    def is_mine(slot):
-        return (y == x) & (lax.rem(z + 8 - slot, 8) == head)
-
-    def final_copy(slot):
+        swap_sums(slot).start()
+
+    def deliver(slot, i):
         return remote(
-            done.at[slot], final.at[x, core], f_send.at[slot], f_recv.at[x, core],
-            branch=z * NX + y, head=lax.rem(z + 8 - slot, 8),
+            summed.at[slot, i], landed.at[x, head], f_send.at[slot, i], f_recv.at[x, head],
+            branch=z * NX + i, head=lax.rem(z + 8 - slot, 8),
         )
 
+    def stays(slot, i):
+        return (i == x) & (lax.rem(z + 8 - slot, 8) == head)
+
     def fold(slot):
-        halve(2, slot).wait_recv()
-        done[slot] = (summed[slot, 4 + upper].astype(F32) + met[slot, 6].astype(F32)).astype(BF)
-        mine_too = is_mine(slot)
-
-        @pl.when(mine_too)
-        def _():
-            final[x, core] = done[slot]
-
-        @pl.when(~mine_too)
-        def _():
-            final_copy(slot).start()
+        swap_sums(slot).wait_recv()
+        for i in range(NX):
+            both = (made[slot, core, i].astype(F32) + met[slot, i].astype(F32)).astype(BF)
+            summed[slot, i] = both
+            here = stays(slot, i)
+
+            @pl.when(here)
+            def _(both=both):
+                landed[x, head] = both
+
+            @pl.when(~here)
+            def _(i=i):
+                deliver(slot, i).start()
 
     order = (0, 1, 7, 2, 6, 3, 5, 4)
 
     def turn(slot):
         n = order.index(slot)
         multiply(slot)
-        for lag, step in ((1, fold_core), (2, fold_near), (3, fold)):
-            if n >= lag:
-                step(order[n - lag])
+        if n >= 1:
+            fold(order[n - 1])
 
     turn(0)
     for k in (1, 2, 3):
@@ -458,34 +430,35 @@
     hop(0, 4, 0).wait_recv()
     hop(1, 4, 1).wait_recv()
     turn(4)
-    fold_core(4)
-    fold_near(5)
-    fold(3)
-    fold_near(4)
-    fold(5)
     fold(4)
 
     for i in range(NX):
+        sides = []
         for n in range(2):
-
-            @pl.when((i != x) | (2 * x + n != head))
-            def _(i=i, n=n):
-                remote(
-                    done.at[0], final.at[i, n], f_send.at[0], f_recv.at[i, n], branch=z * NX + i, head=2 * x + n
-                ).wait_recv()
-
-        out[i * ROWS:(i + 1) * ROWS, :] = jnp.concatenate([final[i, 0][:, :SLICE], final[i, 1][:, :SLICE]], axis=1)
+            acc = jnp.zeros((ROWS, PADDED), F32)
+            for yy in range(NY):
+                src = 2 * yy + n
+
+                @pl.when((i != x) | (src != head))
+                def _(i=i, src=src):
+                    remote(
+                        summed.at[0, 0], landed.at[i, src], f_send.at[0, 0], f_recv.at[i, src],
+                        branch=z * NX + i, head=src,
+                    ).wait_recv()
+
+                acc = acc + landed[i, src].astype(F32)
+            sides.append(acc.astype(BF)[:, :SLICE])
+        out[i * ROWS:(i + 1) * ROWS, :] = jnp.concatenate(sides, axis=1)
 
     for c in hops:
         c.wait_send()
     for slot in range(8):
-
-        @pl.when(~is_mine(slot))
-        def _(slot=slot):
-            final_copy(slot).wait_send()
-
-        for n in range(3):
-            halve(n, slot).wait_send()
+        swap_sums(slot).wait_send()
+        for i in range(NX):
+
+            @pl.when(~stays(slot, i))
+            def _(slot=slot, i=i):
+                deliver(slot, i).wait_send()
 
 
 def layer(*operands):
@@ -521,14 +494,13 @@
             vmem((PAIRS, WIDTH, BLOCK), BF),
             vmem((8, ROWS, HEADS * VDIM), BF),
             vmem((8, 2, NY, ROWS, PADDED), BF),
-            vmem((8, 7, ROWS, PADDED), BF),
-            vmem((8, 6, ROWS, PADDED), BF),
-            vmem((8, ROWS, PADDED), BF),
-            vmem((NX, 2, ROWS, PADDED), BF),
+            vmem((8, NX, ROWS, PADDED), BF),
+            vmem((8, NX, ROWS, PADDED), BF),
+            vmem((NX, 8, ROWS, PADDED), BF),
             dma((13,)), dma,
             dma((GROUPS,)), dma((GROUPS,)), dma((GROUPS,)), dma((GROUPS,)),
             dma((2, 4)), dma((2, 4)), dma((2, 5)), dma((2, 5)),
-            dma((6,)), dma((6,)), dma((2, 4, 2)), dma((2, 4, 2)), dma((3, 8)), dma((3, 8)), dma((8,)), dma((NX, 2)),
+            dma((6,)), dma((6,)), dma((2, 4, 2)), dma((2, 4, 2)), dma((8,)), dma((8,)), dma((8, NX)), dma((NX, 8)),
         ],
         compiler_params=pltpu.CompilerParams(
             collective_id=0, has_side_effects=True, vmem_limit_bytes=VMEM_BYTES

time: 105 us -> 96 us (0.914); the launches traced: 105 us -> 94.9 us
  Pallas kernels: 103 us -> 93.2 us
    pallas_call x1, Pallas kernels: 103 us -> 93.2 us  [layer(): pl.pallas_call(layer_kernel, out_shape=jax.ShapeDtypeStruct((NX * ROWS, C...]
where the time goes in v6:
time: 96 us; the launch traced here: 94.9 us
  Pallas kernels  93.2 us (97%)
  local copies, waits for them, and re-layouts  1.73 us (2%)
    pallas_call x1, Pallas kernels, layer(): pl.pallas_call(layer_kernel, out_shape=jax.ShapeDtypeStruct((NX * ROWS, C...  93.2 us

profile of v6, /device:TPU:18, one launch (start us, length us, event | category | flops | bytes accessed | tf_op | source)
XLA Modules:
  0.0 94.9 jit_solution(4871855148977099895)
XLA Ops:
  0.0 93.2 %shard_map.109 = bf16[384,224]{1,0:T(8,128)(2,1)} custom-call(s32[24]{0:T(128)} %par_hbm.1, s32[24]{0:T(128)} %lens_hbm.1, s32[24]{0:T(128)} %bitcast.7, bf16[96,2048]{1,0:T(8,128)(2,1)} %qn_hbm.1, bf16[96,1024]{1,0:T(8,128)(2,1)} %qr_hbm.1, bf16[16,128,512]{2,1,0:T(8,128)(2,1)} %ku_hbm.1, bf16[16,512,128]{2,1,0:T(8,128)(2,1)} %vu_hbm.1, ...), custom_call_target="tpu_custom_call" | custom-call | flops 4200000000 | bytes 16000000 | tf_op jit(solution)/shard_map/pallas_call | solution.py:467
  93.2 1.7 %copy.12 = bf16[384,224]{0,1:T(8,128)(2,1)} copy(bf16[384,224]{1,0:T(8,128)(2,1)} %shard_map.109) | data formatting | bytes 344064 | tf_op jit(solution)/shard_map/pallas_call | solution.py:467

commit v7 on v6

--- a/solution.py
+++ b/solution.py
@@ -29,7 +29,8 @@
 PADDED = 128
 VMEM_BYTES = 60 * 2**20
 LANES = LAT // 128
-TOGETHER = 1
+TOGETHER = 3
+EARLY = 20
 SCALE = (NOPE + ROPE) ** -0.5
 BF = jnp.bfloat16
 F32 = jnp.float32
@@ -230,7 +231,7 @@
             ctx[j, rows, :] = c[:, j * 128:(j + 1) * 128]
         return 0
 
-    lax.fori_loop(0, B_DEV // 2, prefix, 0)
+    lax.fori_loop(0, EARLY, prefix, 0)
 
     from_down, from_up, from_far = down * 2 + core, up * 2 + core, far * 2 + core
     other = 1 - core
@@ -286,7 +287,7 @@
                     parts[head, p] = slots[par[2 * p] // B_DEV]
                 ring_first(ch, SIZES[c])
 
-    lax.fori_loop(B_DEV // 2, B_DEV, prefix, 0)
+    lax.fori_loop(EARLY, B_DEV, prefix, 0)
 
     for c in range(2):
 
@@ -373,15 +374,17 @@
     share(4, lax.rem(x + 2, NX), 0, right).wait()
     share(5, lax.rem(x + 2, NX), 1, left).wait()
 
-    def swap_sums(slot):
-        return remote(made.at[slot, other], met.at[slot], r_send.at[slot], r_recv.at[slot], head=y * 2 + other)
+    def swap_sums(slot, i):
+        return remote(
+            made.at[slot, other, i], met.at[slot, i], r_send.at[slot, i], r_recv.at[slot, i], head=y * 2 + other
+        )
 
     def multiply(slot):
         for i in range(NX):
             r = dot_nt(held[slot], wt[i * 2 * PADDED:(i + 1) * 2 * PADDED]).astype(BF)
             for n in range(2):
                 made[slot, n, i] = r[:, n * PADDED:(n + 1) * PADDED]
-        swap_sums(slot).start()
+            swap_sums(slot, i).start()
 
     def deliver(slot, i):
         return remote(
@@ -393,8 +396,8 @@
         return (i == x) & (lax.rem(z + 8 - slot, 8) == head)
 
     def fold(slot):
-        swap_sums(slot).wait_recv()
         for i in range(NX):
+            swap_sums(slot, i).wait_recv()
             both = (made[slot, core, i].astype(F32) + met[slot, i].astype(F32)).astype(BF)
             summed[slot, i] = both
             here = stays(slot, i)
@@ -412,7 +415,7 @@
     def turn(slot):
         n = order.index(slot)
         multiply(slot)
-        if n >= 1:
+        if 1 <= n < 7:
             fold(order[n - 1])
 
     turn(0)
@@ -427,6 +430,7 @@
                 turn(9 - k)
         turn(k)
     turn(5)
+    fold(5)
     hop(0, 4, 0).wait_recv()
     hop(1, 4, 1).wait_recv()
     turn(4)
@@ -453,8 +457,8 @@
     for c in hops:
         c.wait_send()
     for slot in range(8):
-        swap_sums(slot).wait_send()
         for i in range(NX):
+            swap_sums(slot, i).wait_send()
 
             @pl.when(~stays(slot, i))
             def _(slot=slot, i=i):
@@ -500,7 +504,7 @@
             dma((13,)), dma,
             dma((GROUPS,)), dma((GROUPS,)), dma((GROUPS,)), dma((GROUPS,)),
             dma((2, 4)), dma((2, 4)), dma((2, 5)), dma((2, 5)),
-            dma((6,)), dma((6,)), dma((2, 4, 2)), dma((2, 4, 2)), dma((8,)), dma((8,)), dma((8, NX)), dma((NX, 8)),
+            dma((6,)), dma((6,)), dma((2, 4, 2)), dma((2, 4, 2)), dma((8, NX)), dma((8, NX)), dma((8, NX)), dma((NX, 8)),
         ],
         compiler_params=pltpu.CompilerParams(
             collective_id=0, has_side_effects=True, vmem_limit_bytes=VMEM_BYTES

time: 96 us -> 98 us (1.021)
  Pallas kernels: 93.2 us -> 95.7 us
    pallas_call x1, Pallas kernels: 93.2 us -> 95.7 us  [layer(): pl.pallas_call(layer_kernel, out_shape=jax.ShapeDtypeStruct((NX * ROWS, C...]
where the time goes in v7:
time: 98 us; the launch traced here: 97.4 us
  Pallas kernels  95.7 us (98%)
  local copies, waits for them, and re-layouts  1.73 us (2%)
    pallas_call x1, Pallas kernels, layer(): pl.pallas_call(layer_kernel, out_shape=jax.ShapeDtypeStruct((NX * ROWS, C...  95.7 us

profile of v7, /device:TPU:18, one launch (start us, length us, event | category | flops | bytes accessed | tf_op | source)
XLA Modules:
  0.0 97.4 jit_solution(13133078145078956026)
XLA Ops:
  0.0 95.7 %shard_map.109 = bf16[384,224]{1,0:T(8,128)(2,1)} custom-call(s32[24]{0:T(128)} %par_hbm.1, s32[24]{0:T(128)} %lens_hbm.1, s32[24]{0:T(128)} %bitcast.7, bf16[96,2048]{1,0:T(8,128)(2,1)} %qn_hbm.1, bf16[96,1024]{1,0:T(8,128)(2,1)} %qr_hbm.1, bf16[16,128,512]{2,1,0:T(8,128)(2,1)} %ku_hbm.1, bf16[16,512,128]{2,1,0:T(8,128)(2,1)} %vu_hbm.1, ...), custom_call_target="tpu_custom_call" | custom-call | flops 4200000000 | bytes 16000000 | tf_op jit(solution)/shard_map/pallas_call | solution.py:471
  95.7 1.7 %copy.12 = bf16[384,224]{0,1:T(8,128)(2,1)} copy(bf16[384,224]{1,0:T(8,128)(2,1)} %shard_map.109) | data formatting | bytes 344064 | tf_op jit(solution)/shard_map/pallas_call | solution.py:471

commit v8 on v6

--- a/solution.py
+++ b/solution.py
@@ -29,7 +29,8 @@
 PADDED = 128
 VMEM_BYTES = 60 * 2**20
 LANES = LAT // 128
-TOGETHER = 1
+TOGETHER = 3
+EARLY = 20
 SCALE = (NOPE + ROPE) ** -0.5
 BF = jnp.bfloat16
 F32 = jnp.float32
@@ -230,7 +231,7 @@
             ctx[j, rows, :] = c[:, j * 128:(j + 1) * 128]
         return 0
 
-    lax.fori_loop(0, B_DEV // 2, prefix, 0)
+    lax.fori_loop(0, EARLY, prefix, 0)
 
     from_down, from_up, from_far = down * 2 + core, up * 2 + core, far * 2 + core
     other = 1 - core
@@ -286,7 +287,7 @@
                     parts[head, p] = slots[par[2 * p] // B_DEV]
                 ring_first(ch, SIZES[c])
 
-    lax.fori_loop(B_DEV // 2, B_DEV, prefix, 0)
+    lax.fori_loop(EARLY, B_DEV, prefix, 0)
 
     for c in range(2):
 
@@ -412,7 +413,7 @@
     def turn(slot):
         n = order.index(slot)
         multiply(slot)
-        if n >= 1:
+        if 1 <= n < 7:
             fold(order[n - 1])
 
     turn(0)
@@ -427,6 +428,7 @@
                 turn(9 - k)
         turn(k)
     turn(5)
+    fold(5)
     hop(0, 4, 0).wait_recv()
     hop(1, 4, 1).wait_recv()
     turn(4)

time: 96 us -> 95.5 us (level)
  no operation moved by 1% of the time
where the time goes in v8:
time: 95.5 us; the launch traced here: 94.2 us
  Pallas kernels  92.5 us (97%)
  local copies, waits for them, and re-layouts  1.73 us (2%)
    pallas_call x1, Pallas kernels, layer(): pl.pallas_call(layer_kernel, out_shape=jax.ShapeDtypeStruct((NX * ROWS, C...  92.5 us

profile of v8, /device:TPU:18, one launch (start us, length us, event | category | flops | bytes accessed | tf_op | source)
XLA Modules:
  0.0 94.2 jit_solution(5968375762282947912)
XLA Ops:
  0.0 92.5 %shard_map.109 = bf16[384,224]{1,0:T(8,128)(2,1)} custom-call(s32[24]{0:T(128)} %par_hbm.1, s32[24]{0:T(128)} %lens_hbm.1, s32[24]{0:T(128)} %bitcast.7, bf16[96,2048]{1,0:T(8,128)(2,1)} %qn_hbm.1, bf16[96,1024]{1,0:T(8,128)(2,1)} %qr_hbm.1, bf16[16,128,512]{2,1,0:T(8,128)(2,1)} %ku_hbm.1, bf16[16,512,128]{2,1,0:T(8,128)(2,1)} %vu_hbm.1, ...), custom_call_target="tpu_custom_call" | custom-call | flops 4200000000 | bytes 16000000 | tf_op jit(solution)/shard_map/pallas_call | solution.py:469
  92.5 1.7 %copy.12 = bf16[384,224]{0,1:T(8,128)(2,1)} copy(bf16[384,224]{1,0:T(8,128)(2,1)} %shard_map.109) | data formatting | bytes 344064 | tf_op jit(solution)/shard_map/pallas_call | solution.py:469
